TPU v7x, 32 devices: a whole 2x2x4 slice. The times are simulated.
32 devices in a mesh: dp: 4 (over y, core), expert: 8 (over z, x).
Axes of the slice: x: 2, y: 2, z: 4, core: 2. Of those that a mesh axis runs over, the one named last changes fastest.
Arguments:
- tokens: bfloat16 [16384, 768], P(('dp', 'expert')), may hold values from -6 to 6
- segments: int32 [32, 512], P(('dp', 'expert')), may hold values from 0 to 4, never falling along the last dimension, each value on 1 to 256 neighbouring positions
- routes: int32 [16384], P(('dp', 'expert')), may hold values from 0 to 15
- slots: int32 [16384], P(('dp', 'expert')), may hold values from -1 to 39, as said below
- bucket_table: int32 [1023], replicated, may hold values from 0 to 31
- gain_attn: float32 [768], replicated, may hold values from 0.1 to 1.9
- w_query: bfloat16 [768, 768], P('dp'), may hold values from -0.21875 to 0.21875
- w_key: bfloat16 [768, 768], P('dp'), may hold values from -0.21875 to 0.21875
- w_value: bfloat16 [768, 768], P('dp'), may hold values from -0.21875 to 0.21875
- w_output: bfloat16 [768, 768], P('dp'), may hold values from -0.625 to 0.625
- rel_bias: float32 [32, 12], replicated, may hold values from -4 to 4
- gain_ffn: float32 [768], replicated, may hold values from 0.1 to 1.9
- w_router: bfloat16 [768, 16], P('dp'), may hold values from -0.15625 to 0.15625
- w_in: bfloat16 [16, 768, 3072], P('expert'), may hold values from -0.21875 to 0.21875
- w_out: bfloat16 [16, 3072, 768], P('expert'), may hold values from -1.75 to 1.75
- cotangent: bfloat16 [16384, 768], P(('dp', 'expert')), may hold values from -6 to 6
Outputs:
- output: bfloat16 [16384, 768], P(('dp', 'expert'))
- grad_tokens: float32 [16384, 768], P(('dp', 'expert'))
- grad_gain_attn: float32 [768], replicated
- grad_query: float32 [768, 768], P('dp')
- grad_key: float32 [768, 768], P('dp')
- grad_value: float32 [768, 768], P('dp')
- grad_output: float32 [768, 768], P('dp')
- grad_rel_bias: float32 [32, 12], replicated
- grad_gain_ffn: float32 [768], replicated
- grad_router: float32 [768, 16], P('dp')
- grad_w_in: float32 [16, 768, 3072], P('expert', None, 'dp')
- grad_w_out: float32 [16, 3072, 768], P('expert', 'dp')
Inputs may be any that keep to these rules, and one draw needn't show every extreme that they name: `slots`: a token's slot is the number of earlier tokens of its device with the same route when that number is under 40, and -1 otherwise.
All inputs are finite; a program needn't handle non-finite values.
Results may differ from a plain program's by a relative error of at most 0.02.
Values may be sent and summed in bfloat16 or wider, within the bound.
No kernel may reach another device: no remote copies, remote signals or barrier semaphores. Data moves between devices by JAX's collectives and lax.ppermute only.
A program may use at most 256 MiB of HBM per device.

v0:
```python
import math

import jax
import jax.numpy as jnp
from jax import lax
from jax.sharding import PartitionSpec as P

EPS = 1e-06
HIGH = lax.Precision.HIGHEST


def rms_scale(stream):
    return lax.rsqrt(jnp.mean(stream * stream, axis=-1, keepdims=True) + EPS)


def norm_back(stream, scale, gain, grad_out):
    grad_gain = jnp.sum(grad_out * stream * scale, axis=0)
    scaled = grad_out * gain
    grad_in = scale * scaled - stream * (scale * scale * scale) * jnp.mean(
        scaled * stream, axis=-1, keepdims=True
    )
    return (grad_in, grad_gain)


def toeplitz_bias(relative_t, length):
    head_count = relative_t.shape[0]
    padded = jnp.pad(relative_t, ((0, 0), (0, 1)))
    tiled = jnp.tile(padded, (1, length))
    window = tiled[:, length - 1 : length - 1 + length * (2 * length - 1)]
    return window.reshape(head_count, length, 2 * length - 1)[:, :, :length]


def block_scores(query_blk, key_h, bias_blk, same_doc, factor):
    scores = (
        jnp.einsum("ihd,jhd->hij", query_blk, key_h, preferred_element_type=jnp.float32) * factor
        + bias_blk
    )
    return jnp.where(same_doc[None], scores, -1000000000.0)


def diagonal_sums(grad_scores):
    head_count, row_count, col_count = grad_scores.shape
    width = col_count + row_count
    padded = jnp.pad(grad_scores, ((0, 0), (0, 0), (row_count, 0)))
    flat_rows = padded.reshape(head_count, row_count * width)
    flat_rows = jnp.pad(flat_rows, ((0, 0), (0, row_count)))
    sheared = flat_rows.reshape(head_count, row_count, width + 1)
    diag_sums = jnp.sum(sheared, axis=1, dtype=jnp.float32)[:, 1:width]
    return diag_sums


def body(
    tokens,
    segments,
    routes,
    slots,
    bucket_table,
    gain_attn,
    w_query,
    w_key,
    w_value,
    w_output,
    rel_bias,
    gain_ffn,
    w_router,
    w_in,
    w_out,
    cotangent,
):
    seq_len, model_width = tokens.shape
    head_count = rel_bias.shape[1]
    head_dim = model_width // head_count
    factor = 1.0 / math.sqrt(head_dim)
    block_len = min(512, seq_len)
    starts = list(range(0, seq_len, block_len))
    full_q, full_k, full_v, full_o, full_r = (
        lax.all_gather(w_query, "dp", axis=0, tiled=True),
        lax.all_gather(w_key, "dp", axis=0, tiled=True),
        lax.all_gather(w_value, "dp", axis=0, tiled=True),
        lax.all_gather(w_output, "dp", axis=0, tiled=True),
        lax.all_gather(w_router, "dp", axis=0, tiled=True),
    )
    doc_ids = segments[0]
    same_doc = doc_ids[:, None] == doc_ids[None, :]
    table_hot = (
        bucket_table[:, None] == jnp.arange(rel_bias.shape[0], dtype=jnp.int32)[None, :]
    ).astype(jnp.float32)
    relative_t = jnp.dot(table_hot, rel_bias, precision=HIGH).T
    pos_bias = toeplitz_bias(relative_t, seq_len)
    stream = tokens.astype(jnp.float32)
    scale_one = rms_scale(stream)
    normed_b = (stream * scale_one * gain_attn).astype(jnp.bfloat16)
    queries = jnp.dot(normed_b, full_q, preferred_element_type=jnp.float32).astype(jnp.bfloat16)
    key_rows = jnp.dot(normed_b, full_k, preferred_element_type=jnp.float32).astype(jnp.bfloat16)
    value_rows = jnp.dot(normed_b, full_v, preferred_element_type=jnp.float32).astype(jnp.bfloat16)
    query_h = queries.reshape(seq_len, head_count, head_dim)
    key_h = key_rows.reshape(seq_len, head_count, head_dim)
    value_h = value_rows.reshape(seq_len, head_count, head_dim)
    lse_parts = []
    context_parts = []
    for row_start in starts:
        scores = block_scores(query_h, key_h, pos_bias, same_doc, factor)
        row_peak = jnp.max(scores, axis=-1, keepdims=True)
        log_total = row_peak + jnp.log(jnp.sum(jnp.exp(scores - row_peak), axis=-1, keepdims=True))
        weights = jnp.exp(scores - log_total).astype(jnp.bfloat16)
        context_parts.append(
            jnp.einsum(
                "hij,jhd->ihd", weights, value_h, preferred_element_type=jnp.float32
            ).reshape(block_len, model_width)
        )
        lse_parts.append(log_total)
    context_b = context_parts[0].astype(jnp.bfloat16)
    middle = stream + jnp.dot(context_b, full_o, preferred_element_type=jnp.float32)
    scale_two = rms_scale(middle)
    normed_two = (middle * scale_two * gain_ffn).astype(jnp.bfloat16)
    logits = jnp.dot(normed_two, full_r, preferred_element_type=jnp.float32)
    experts = full_r.shape[1]
    router_p = jax.nn.softmax(logits, axis=-1)
    route_hot = (routes[:, None] == jnp.arange(experts, dtype=jnp.int32)[None, :]).astype(
        jnp.float32
    )
    gate_prob = jnp.sum(router_p * route_hot, axis=-1)
    capacity = max(2, (5 * seq_len + 4 * experts - 1) // (4 * experts))
    local_experts = w_in.shape[0]
    peer_count = lax.axis_size("expert")
    target = jnp.where(slots >= 0, routes * capacity + slots, experts * capacity)

    def to_slots(row_values):
        placed = (
            jnp.zeros((experts * capacity, model_width), jnp.bfloat16)
            .at[target]
            .set(row_values, mode="drop")
        )
        return placed.reshape(peer_count, local_experts * capacity, model_width)

    def from_slots(arrived):
        flat_rows = arrived.reshape(experts * capacity, model_width)
        return jnp.take(flat_rows, target, axis=0, mode="fill", fill_value=0).astype(jnp.float32)

    received = lax.all_to_all(
        to_slots(normed_two), "expert", split_axis=0, concat_axis=0, tiled=True
    )
    received = received.reshape(peer_count, local_experts, capacity, model_width)
    pre_act = jnp.einsum("slcd,ldf->slcf", received, w_in, preferred_element_type=jnp.float32)
    hidden_b = jax.nn.gelu(pre_act).astype(jnp.bfloat16)
    produced = jnp.einsum(
        "slcf,lfd->slcd", hidden_b, w_out, preferred_element_type=jnp.float32
    ).astype(jnp.bfloat16)
    came_back = lax.all_to_all(
        produced.reshape(peer_count, local_experts * capacity, model_width),
        "expert",
        split_axis=0,
        concat_axis=0,
        tiled=True,
    )
    returned = from_slots(came_back)
    output = (middle + gate_prob[:, None] * returned).astype(jnp.bfloat16)
    grad_stream = cotangent.astype(jnp.float32)
    grad_returned = (gate_prob[:, None] * grad_stream).astype(jnp.bfloat16)
    grad_gate = jnp.sum(grad_stream * returned, axis=-1)
    grad_produced = lax.all_to_all(
        to_slots(grad_returned), "expert", split_axis=0, concat_axis=0, tiled=True
    )
    grad_produced = grad_produced.reshape(peer_count, local_experts, capacity, model_width)
    grad_hidden = jnp.einsum(
        "slcd,lfd->slcf", grad_produced, w_out, preferred_element_type=jnp.float32
    )
    grad_pre = jax.vjp(jax.nn.gelu, pre_act)[1](grad_hidden)[0].astype(jnp.bfloat16)
    grad_received = jnp.einsum(
        "slcf,ldf->slcd", grad_pre, w_in, preferred_element_type=jnp.float32
    ).astype(jnp.bfloat16)
    grad_back = lax.all_to_all(
        grad_received.reshape(peer_count, local_experts * capacity, model_width),
        "expert",
        split_axis=0,
        concat_axis=0,
        tiled=True,
    )
    grad_routed = from_slots(grad_back)
    grad_w_out = jnp.einsum(
        "slcf,slcd->lfd", hidden_b, grad_produced, preferred_element_type=jnp.float32
    )
    grad_w_in = jnp.einsum("slcd,slcf->ldf", received, grad_pre, preferred_element_type=jnp.float32)
    grad_in_shard, grad_out_shard = (
        lax.psum_scatter(
            grad_w_in.astype(jnp.bfloat16), "dp", scatter_dimension=2, tiled=True
        ).astype(jnp.float32),
        lax.psum_scatter(
            grad_w_out.astype(jnp.bfloat16), "dp", scatter_dimension=1, tiled=True
        ).astype(jnp.float32),
    )
    grad_logits = (
        router_p * (route_hot * grad_gate[:, None] - (gate_prob * grad_gate)[:, None])
    ).astype(jnp.bfloat16)
    grad_router = jnp.dot(normed_two.T, grad_logits, preferred_element_type=jnp.float32)
    grad_normed_two = (
        jnp.dot(grad_logits, full_r.T, preferred_element_type=jnp.float32) + grad_routed
    )
    grad_mid_norm, grad_gain_two = norm_back(middle, scale_two, gain_ffn, grad_normed_two)
    grad_middle = grad_stream + grad_mid_norm
    grad_attn = grad_middle.astype(jnp.bfloat16)
    grad_w_output = jnp.dot(context_b.T, grad_attn, preferred_element_type=jnp.float32)
    grad_context = jnp.dot(grad_attn, full_o.T, preferred_element_type=jnp.float32).astype(
        jnp.bfloat16
    )
    grad_context = grad_context.reshape(seq_len, head_count, head_dim)
    grad_keys = jnp.zeros((seq_len, head_count, head_dim), jnp.float32)
    grad_values = jnp.zeros((seq_len, head_count, head_dim), jnp.float32)
    grad_relative = jnp.zeros((head_count, 2 * seq_len - 1), jnp.float32)
    grad_query_parts = []
    for block_num, row_start in enumerate(starts):
        scores = block_scores(query_h, key_h, pos_bias, same_doc, factor)
        weights_f = jnp.exp(scores - lse_parts[block_num])
        weights_b = weights_f.astype(jnp.bfloat16)
        grad_values = jnp.einsum(
            "hij,ihd->jhd", weights_b, grad_context, preferred_element_type=jnp.float32
        )
        grad_weights = jnp.einsum(
            "ihd,jhd->hij", grad_context, value_h, preferred_element_type=jnp.float32
        )
        grad_scores = weights_f * (
            grad_weights - jnp.sum(grad_weights * weights_f, axis=-1, keepdims=True)
        )
        grad_scores_b = grad_scores.astype(jnp.bfloat16)
        grad_query_parts.append(
            jnp.einsum("hij,jhd->ihd", grad_scores_b, key_h, preferred_element_type=jnp.float32)
            * factor
        )
        grad_keys = (
            jnp.einsum("hij,ihd->jhd", grad_scores_b, query_h, preferred_element_type=jnp.float32)
            * factor
        )
        grad_relative = diagonal_sums(grad_scores_b)
    grad_q_b = grad_query_parts[0].reshape(seq_len, model_width).astype(jnp.bfloat16)
    grad_k_b = grad_keys.reshape(seq_len, model_width).astype(jnp.bfloat16)
    grad_v_b = grad_values.reshape(seq_len, model_width).astype(jnp.bfloat16)
    grad_w_query = jnp.dot(normed_b.T, grad_q_b, preferred_element_type=jnp.float32)
    grad_w_key = jnp.dot(normed_b.T, grad_k_b, preferred_element_type=jnp.float32)
    grad_w_value = jnp.dot(normed_b.T, grad_v_b, preferred_element_type=jnp.float32)
    grad_normed = jnp.dot(grad_q_b, full_q.T, preferred_element_type=jnp.float32)
    grad_normed = grad_normed + jnp.dot(grad_k_b, full_k.T, preferred_element_type=jnp.float32)
    grad_normed = grad_normed + jnp.dot(grad_v_b, full_v.T, preferred_element_type=jnp.float32)
    grad_first, grad_gain_one = norm_back(stream, scale_one, gain_attn, grad_normed)
    grad_tokens = grad_middle + grad_first
    grad_rel = jnp.dot(grad_relative, table_hot, precision=HIGH).T
    dense_terms = (grad_w_query, grad_w_key, grad_w_value, grad_w_output, grad_router)
    summed = (
        lax.psum(dense_terms[0].astype(jnp.bfloat16), "expert").astype(jnp.float32),
        lax.psum(dense_terms[1].astype(jnp.bfloat16), "expert").astype(jnp.float32),
        lax.psum(dense_terms[2].astype(jnp.bfloat16), "expert").astype(jnp.float32),
        lax.psum(dense_terms[3].astype(jnp.bfloat16), "expert").astype(jnp.float32),
        lax.psum(dense_terms[4].astype(jnp.bfloat16), "expert").astype(jnp.float32),
    )
    shard_q, shard_k, shard_v, shard_o, shard_r = (
        lax.psum_scatter(
            summed[0].astype(jnp.bfloat16), "dp", scatter_dimension=0, tiled=True
        ).astype(jnp.float32),
        lax.psum_scatter(
            summed[1].astype(jnp.bfloat16), "dp", scatter_dimension=0, tiled=True
        ).astype(jnp.float32),
        lax.psum_scatter(
            summed[2].astype(jnp.bfloat16), "dp", scatter_dimension=0, tiled=True
        ).astype(jnp.float32),
        lax.psum_scatter(
            summed[3].astype(jnp.bfloat16), "dp", scatter_dimension=0, tiled=True
        ).astype(jnp.float32),
        lax.psum_scatter(
            summed[4].astype(jnp.bfloat16), "dp", scatter_dimension=0, tiled=True
        ).astype(jnp.float32),
    )
    total_gain_one, total_gain_two, total_rel = lax.psum(
        (grad_gain_one, grad_gain_two, grad_rel), ("dp", "expert")
    )
    return (
        output,
        grad_tokens,
        total_gain_one,
        shard_q,
        shard_k,
        shard_v,
        shard_o,
        total_rel,
        total_gain_two,
        shard_r,
        grad_in_shard,
        grad_out_shard,
    )


def solution(mesh):
    in_specs = (
        P(("dp", "expert"), None),
        P(("dp", "expert"), None),
        P(("dp", "expert")),
        P(("dp", "expert")),
        P(),
        P(),
        P("dp", None),
        P("dp", None),
        P("dp", None),
        P("dp", None),
        P(),
        P(),
        P("dp", None),
        P("expert", None, None),
        P("expert", None, None),
        P(("dp", "expert"), None),
    )
    out_specs = (
        P(("dp", "expert"), None),
        P(("dp", "expert"), None),
        P(),
        P("dp", None),
        P("dp", None),
        P("dp", None),
        P("dp", None),
        P(),
        P(),
        P("dp", None),
        P("expert", None, "dp"),
        P("expert", "dp", None),
    )
    return jax.shard_map(body, mesh=mesh, in_specs=in_specs, out_specs=out_specs, check_vma=False)
```

profile of v0, /device:TPU:0, one launch (start us, length us, event | category | flops | bytes accessed | tf_op | source)
XLA Modules:
  0.0 726.3 jit_solution(1091719539078631305)
XLA Ops:
  12.7 11.9 %tile.4 = f32[12,512,1024]{2,1,0:T(8,128)} broadcast(f32[12,1024]{1,0:T(8,128)S(1)} %pad.12), dimensions={0,2} | broadcast | bytes 25214976 | tf_op jit(solution)/shard_map/tile | solution.py:28
  24.6 11.0 %pad.17 = f32[16,512,1024]{2,1,0:T(8,128)S(1)} pad(f32[12,512,1024]{2,1,0:T(8,128)} %tile.4, f32[]{:T(128)} %constant.24.clone.1), padding=0_4x0_0x0_0 | pad | bytes 58720260
  35.6 39.7 %copy.85 = f32[2,8,512,1024]{3,1,2,0:T(8,128)} copy(f32[2,8,512,1024]{3,2,1,0:T(8,128)S(1)} %bitcast.133) | data formatting | bytes 67108864
  75.3 25.8 %slice.16 = f32[12,523776]{1,0:T(8,128)} slice(f32[12,524288]{1,0:T(8,128)} %bitcast.134), slice={[0:12], [511:524287]} | slice | bytes 50282496 | tf_op jit(solution)/shard_map/slice | solution.py:29
  101.2 49.2 %reshape.178 = f32[12,512,1023]{2,1,0:T(8,128)} reshape(f32[12,523776]{1,0:T(8,128)} %slice.16) | data formatting | bytes 50282496 | tf_op jit(solution)/shard_map/reshape | solution.py:30
  150.4 10.7 %slice.17 = f32[12,512,512]{2,1,0:T(8,128)} slice(f32[12,512,1023]{2,1,0:T(8,128)} %reshape.178), slice={[0:12], [0:512], [0:512]} | slice | bytes 25165824 | tf_op jit(solution)/shard_map/slice | solution.py:30
  161.1 12.7 %copy.83 = f32[12,512,512]{1,2,0:T(8,128)} copy(f32[12,512,512]{2,1,0:T(8,128)} %slice.17) | data formatting | bytes 25165824
  174.4 2.1 convolution_convert_fusion.6
  176.8 2.4 convolution_convert_fusion.5
  179.5 9.1 %fusion.83 = (f32[12,512]{1,0:T(8,128)S(1)}, f32[12,512,512]{1,2,0:T(8,128)}) fusion(f32[12,512,512]{1,2,0:T(8,128)} %copy.83, bf16[512,12,64]{0,2,1:T(8,128)(2,1)S(1)} %bitcast.147, bf16[512,12,64]{0,2,1:T(8,128)(2,1)S(1)} %bitcast.139, pred[512,512]{0,1:T(8,128)(4,1)S(1)} %broadcast_compare_fusion), kind=kOutput, calls=%fused_computation.120 | convolution fusion | flops 415229952 | bytes 27025408 | tf_op jit(solution)/shard_map/ihd,jhd->hij/dot_general | solution.py:35
  188.6 2.1 convolution_convert_fusion.7
  191.1 6.9 exponential_reduce_fusion
  199.5 3.0 fusion.46
  202.5 2.5 multiply_reduce_fusion.3
  205.5 4.0 scatter_custom_fusion
  209.5 7.0 all-to-all-start
  216.5 5.2 all-gather
  222.5 4.4 scatter_custom_fusion.1
  226.8 14.2 %all-to-all-done = bf16[8,80,768]{2,1,0:T(8,128)(2,1)S(1)} async-done(((bf16[8,80,768]{2,1,0:T(8,128)(2,1)}), bf16[8,80,768]{2,1,0:T(8,128)(2,1)S(1)}, u32[]{:S(2)}, u32[]{:S(2)}) %all-to-all-start) | async-done | bytes 983072 | tf_op jit(solution)/shard_map/all_to_all | solution.py:140
  241.0 4.2 all-to-all-start.2
  245.3 5.8 fusion.3
  251.1 10.6 %fusion.55 = bf16[8,2,40,768]{3,2,0,1:T(8,128)(2,1)S(1)} fusion(bf16[2,3072,768]{2,1,0:T(8,128)(2,1)} %param.32, f32[2,8,40,3072]{3,2,1,0:T(8,128)S(1)} %fusion.3), kind=kOutput, calls=%fused_computation.84 | convolution fusion | flops 3038085120 | bytes 18284544 | tf_op jit(solution)/shard_map/slcf,lfd->slcd/dot_general | solution.py:146
  262.7 6.8 all-to-all-done.2
  269.5 4.0 all-to-all-start.1
  273.5 11.1 %fusion.15 = bf16[8,2,40,3072]{3,2,0,1:T(8,128)(2,1)S(1)} fusion(f32[2,8,40,3072]{3,2,1,0:T(8,128)} %copy-done.4, bf16[2,3072,768]{2,1,0:T(8,128)(2,1)} %param.32, bf16[8,2,40,768]{3,2,1,0:T(8,128)(2,1)} %bitcast.19), kind=kOutput, calls=%fused_computation.29 | convolution fusion | flops 3059220480 | bytes 22216704 | tf_op jit(solution)/shard_map/slcd,lfd->slcf/dot_general | solution.py:165
  284.6 8.5 %fusion.52 = bf16[8,2,40,768]{3,2,0,1:T(8,128)(2,1)S(1)} fusion(bf16[8,2,40,3072]{3,2,0,1:T(8,128)(2,1)S(1)} %fusion.15, bf16[2,768,3072]{2,1,0:T(8,128)(2,1)} %param.31), kind=kOutput, calls=%fused_computation.83 | convolution fusion | flops 3020390400 | bytes 14352384 | tf_op jit(solution)/shard_map/slcf,ldf->slcd/dot_general | solution.py:169
  294.1 3.7 all-to-all-done.1
  297.8 3.6 all-to-all-start.3
  302.2 2.7 gather_fusion
  304.9 1.8 fusion.29
  307.4 18.6 %all-to-all-done.3 = bf16[8,80,768]{2,1,0:T(8,128)(2,1)S(1)} async-done(((bf16[8,80,768]{2,1,0:T(8,128)(2,1)}), bf16[8,80,768]{2,1,0:T(8,128)(2,1)S(1)}, u32[]{:S(2)}, u32[]{:S(2)}) %all-to-all-start.3) | async-done | bytes 983072 | tf_op jit(solution)/shard_map/all_to_all | solution.py:172
  326.0 2.3 gather_fusion.1
  329.8 1.6 convert_add_fusion.1
  331.4 1.8 convolution_convert_fusion
  333.5 2.1 convolution_convert_fusion.4
  336.0 7.2 fusion.49
  344.1 2.0 convolution_convert_fusion.1
  346.2 6.3 multiply_reduce_fusion
  352.5 6.3 multiply_convert_fusion
  362.4 2.0 convolution_convert_fusion.3
  364.5 5.0 multiply_convert_fusion.1
  370.4 2.0 convolution_convert_fusion.2
  373.6 12.9 %reduce-scatter.18.cloned.1.call-done = bf16[192,768]{1,0:T(8,128)(2,1)} async-done(((bf16[768,768]{1,0:T(8,128)(2,1)}), bf16[192,768]{1,0:T(8,128)(2,1)}) %reduce-scatter.18.cloned.1.call-update) | async-done | bytes 294928 | tf_op jit(solution)/shard_map/reduce_scatter | solution.py:261
  386.5 28.9 %reduce-scatter.14.cloned.1.call-done = bf16[192,768]{1,0:T(8,128)(2,1)} async-done(((bf16[768,768]{1,0:T(8,128)(2,1)}), bf16[192,768]{1,0:T(8,128)(2,1)}) %reduce-scatter.14.cloned.1.call-update) | async-done | bytes 294928 | tf_op jit(solution)/shard_map/reduce_scatter | solution.py:255
  415.4 29.1 %reduce-scatter.16.cloned.1.call-done = bf16[192,768]{1,0:T(8,128)(2,1)} async-done(((bf16[768,768]{1,0:T(8,128)(2,1)}), bf16[192,768]{1,0:T(8,128)(2,1)}) %reduce-scatter.16.cloned.1.call-update) | async-done | bytes 294928 | tf_op jit(solution)/shard_map/reduce_scatter | solution.py:258
  445.0 10.5 %bitcast_convert_fusion = bf16[2,3072,768]{2,1,0:T(8,128)(2,1)} fusion(bf16[8,2,40,768]{3,2,1,0:T(8,128)(2,1)} %bitcast.19, f32[2,8,40,3072]{3,2,1,0:T(8,128)} %copy-done.4), kind=kOutput, calls=%fused_computation.4 | convolution fusion | flops 3042312192 | bytes 18284544 | tf_op jit(solution)/shard_map/slcf,slcd->lfd/dot_general | solution.py:180
  456.6 9.7 %bitcast_convert_fusion.1 = bf16[2,768,3072]{2,1,0:T(8,128)(2,1)} fusion(bf16[8,2,40,768]{3,2,1,0:T(8,128)(2,1)S(1)} %bitcast.142, bf16[8,2,40,3072]{3,2,0,1:T(8,128)(2,1)} %copy-done.66), kind=kOutput, calls=%fused_computation.5 | convolution fusion | flops 3024617472 | bytes 14352384 | tf_op jit(solution)/shard_map/slcd,slcf->ldf/dot_general | solution.py:183
  466.4 8.7 %copy.84 = bf16[12,512,512]{2,1,0:T(8,128)(2,1)} copy(bf16[12,512,512]{1,2,0:T(8,128)(2,1)} %copy-done.3) | data formatting | bytes 12582912
  475.1 5.1 pad.13.clone
  480.2 2.2 pad.18
  482.4 29.2 %copy.86 = bf16[2,8,512,1024]{3,1,2,0:T(8,128)(2,1)S(1)} copy(bf16[2,8,512,1024]{3,2,1,0:T(8,128)(2,1)S(1)} %bitcast.135) | data formatting | bytes 33554432
  511.6 11.4 %pad_convert_fusion = f32[12,524800]{1,0:T(8,128)} fusion(bf16[12,524288]{1,0:T(8,128)(2,1)S(1)} %bitcast.136), kind=kLoop, calls=%fused_computation.6 | loop fusion | flops 6297600 | bytes 37773312 | tf_op jit(solution)/shard_map/convert_element_type | solution.py:48
  523.0 48.7 %reshape.189 = f32[12,512,1025]{2,1,0:T(8,128)} reshape(f32[12,524800]{1,0:T(8,128)} %pad_convert_fusion) | data formatting | bytes 50380800 | tf_op jit(solution)/shard_map/convert_element_type | solution.py:48
  571.7 10.4 %reduce_sum.118 = f32[12,1025]{1,0:T(8,128)S(1)} reduce(f32[12,512,1025]{2,1,0:T(8,128)} %reshape.189, f32[]{:T(128)} %constant.24.clone.1), dimensions={1}, to_apply=%region_23.25 | reduce | flops 6285300 | bytes 25239604 | tf_op jit(solution)/shard_map/reduce_sum | solution.py:48
  582.6 2.2 fusion.85
  586.4 2.3 fusion.39
  588.7 40.6 %all-reduce.3 = (f32[768]{0:T(1024)}, f32[32,12]{0,1:T(8,128)}, f32[768]{0:T(1024)}) all-reduce(f32[768]{0:T(1024)S(1)} %get-tuple-element.15, f32[32,12]{0,1:T(8,128)S(1)} %fusion.64, f32[768]{0:T(1024)S(1)} %copy-done.53), channel_id=1, replica_groups=mesh['dp'=4,'expert'=8] {'dp','expert'}, use_global_device_ids=true, to_apply=%region_14.16 | all-reduce | flops 1920 | bytes 15360 | tf_op jit(solution)/shard_map/psum | solution.py:271
  629.3 3.0 fusion.36
  633.2 21.3 %psum.68 = bf16[192,16]{0,1:T(8,128)(2,1)S(1)} all-reduce(bf16[192,16]{0,1:T(8,128)(2,1)S(1)} %copy.82), channel_id=1, replica_groups=mesh['dp'=4,'expert'=8] {'expert'}, use_global_device_ids=true, to_apply=%region_27.29 | all-reduce | flops 3072 | bytes 12288 | tf_op jit(solution)/shard_map/psum | solution.py:252
  655.1 1.9 convert_element_type.204
  657.0 1.8 convert_element_type.206
  660.6 4.6 convert_element_type.218
  665.2 49.7 %reduce-scatter.10.cloned.1.call-done = bf16[2,768,768]{2,1,0:T(8,128)(2,1)} async-done(((bf16[2,768,3072]{2,1,0:T(8,128)(2,1)}), bf16[2,768,768]{2,1,0:T(8,128)(2,1)}) %reduce-scatter.10.cloned.1.call-update) | async-done | bytes 2359312 | tf_op jit(solution)/shard_map/reduce_scatter | solution.py:185
  714.8 4.2 convert_element_type.216
  (200 shorter events, 28.5 us)
Async XLA Ops:
  7.2 5.0 copy-start
  7.2 4.8 copy-start.56
  7.2 5.0 copy-start.64
  7.2 167.1 %all-gather.8.cloned.1.call-start = ((), (), s32[]{:S(2)}) async-start(), calls=%async_computation.12 | async-start | bytes 1474560 | tf_op jit(solution)/shard_map/all_gather | solution.py:77
  8.0 168.8 %all-gather.10.cloned.1.call-start = ((), (), s32[]{:S(2)}) async-start(), calls=%async_computation.13 | async-start | bytes 1474560 | tf_op jit(solution)/shard_map/all_gather | solution.py:78
  8.7 179.9 %all-gather.6.cloned.1.call-start = ((), (), s32[]{:S(2)}) async-start(), calls=%async_computation.11 | async-start | bytes 1474560 | tf_op jit(solution)/shard_map/all_gather | solution.py:79
  9.4 193.0 %all-gather.12.cloned.1.call-start = ((), (), s32[]{:S(2)}) async-start(), calls=%async_computation.14 | async-start | bytes 1474560 | tf_op jit(solution)/shard_map/all_gather | solution.py:80
  12.0 176.7 %copy-start.49 = (f32[512]{0:T(512)}, f32[512]{0:T(512)S(1)}, u32[]{:S(2)}) copy-start(f32[512]{0:T(512)S(1)} %get-tuple-element.29) | copy-start | bytes 6148
  161.1 12.8 %copy-start.42 = (s32[512]{0:T(512)S(1)}, s32[512]{0:T(512)}, u32[]{:S(2)}) copy-start(s32[512]{0:T(512)} %param.20) | copy-start | bytes 6148
  161.1 12.8 %copy-start.62 = (s32[512]{0:T(512)S(1)}, s32[512]{0:T(512)}, u32[]{:S(2)}) copy-start(s32[512]{0:T(512)} %param.21) | copy-start | bytes 6148
  161.1 13.3 %copy-start.16 = (bf16[512,768]{1,0:T(8,128)(2,1)S(1)}, bf16[512,768]{1,0:T(8,128)(2,1)}, u32[]{:S(2)}) copy-start(bf16[512,768]{1,0:T(8,128)(2,1)} %param.18) | copy-start | bytes 2359300
  161.1 13.3 %copy-start.51 = (f32[768]{0:T(1024)S(1)}, f32[768]{0:T(1024)}, u32[]{:S(2)}) copy-start(f32[768]{0:T(1024)} %param.23) | copy-start | bytes 9220
  174.3 31.2 %copy-start.60 = (s32[512]{0:T(512)}, s32[512]{0:T(512)S(1)}, u32[]{:S(2)}) copy-start(s32[512]{0:T(512)S(1)} %get-tuple-element.25) | copy-start | bytes 6148
  176.8 2.7 copy-start.11
  179.5 9.1 %copy-start.5 = (bf16[512,768]{0,1:T(8,128)(2,1)}, bf16[512,768]{0,1:T(8,128)(2,1)S(1)}, u32[]{:S(2)}) copy-start(bf16[512,768]{0,1:T(8,128)(2,1)S(1)} %copy.59) | copy-start | bytes 2359300
  191.1 6.9 copy-start.9
  191.1 8.5 %copy-start.2 = (f32[12,512,512]{1,2,0:T(8,128)S(1)}, f32[12,512,512]{1,2,0:T(8,128)}, u32[]{:S(2)}) copy-start(f32[12,512,512]{1,2,0:T(8,128)} %get-tuple-element.33) | copy-start | bytes 37748740
  199.5 3.0 copy-start.17
  202.5 3.1 copy-start.38
  205.5 10.9 %copy-start.59 = (bf16[192,16]{0,1:T(8,128)(2,1)S(1)}, bf16[192,16]{0,1:T(8,128)(2,1)}, u32[]{:S(2)}) copy-start(bf16[192,16]{0,1:T(8,128)(2,1)} %param.30) | copy-start | bytes 18436
  209.5 31.5 %all-to-all-start = ((bf16[8,80,768]{2,1,0:T(8,128)(2,1)}), bf16[8,80,768]{2,1,0:T(8,128)(2,1)S(1)}, u32[]{:S(2)}, u32[]{:S(2)}) async-start(bf16[8,80,768]{2,1,0:T(8,128)(2,1)} %bitcast.8), calls=%async_computation | async-start | bytes 1966080 | tf_op jit(solution)/shard_map/all_to_all | solution.py:140
  221.8 5.0 copy-start.36
  222.0 19.0 %copy-start.13 = (bf16[512,768]{1,0:T(8,128)(2,1)}, bf16[512,768]{1,0:T(8,128)(2,1)S(1)}, u32[]{:S(2)}) copy-start(bf16[512,768]{1,0:T(8,128)(2,1)S(1)} %multiply_convert_fusion.3) | copy-start | bytes 2359300
  222.4 22.9 %copy-start.27 = (f32[512,16]{0,1:T(8,128)}, f32[512,16]{0,1:T(8,128)S(1)}, u32[]{:S(2)}) copy-start(f32[512,16]{0,1:T(8,128)S(1)} %get-tuple-element.37) | copy-start | bytes 98308
  222.4 22.9 %copy-start.39 = (f32[512]{0:T(512)}, f32[512]{0:T(512)S(1)}, u32[]{:S(2)}) copy-start(f32[512]{0:T(512)S(1)} %fusion.74) | copy-start | bytes 6148
  222.5 22.8 %copy-start.45 = (f32[512]{0:T(512)}, f32[512]{0:T(512)S(1)}, u32[]{:S(2)}) copy-start(f32[512]{0:T(512)S(1)} %select_reduce_fusion) | copy-start | bytes 6148
  241.0 10.1 %copy-start.7 = (bf16[8,80,768]{2,1,0:T(8,128)(2,1)}, bf16[8,80,768]{2,1,0:T(8,128)(2,1)S(1)}, u32[]{:S(2)}) copy-start(bf16[8,80,768]{2,1,0:T(8,128)(2,1)S(1)} %all-to-all-done) | copy-start | bytes 2949124
  241.0 28.5 %all-to-all-start.2 = ((bf16[8,80,768]{2,1,0:T(8,128)(2,1)}), bf16[8,80,768]{2,1,0:T(8,128)(2,1)}, u32[]{:S(2)}, u32[]{:S(2)}) async-start(bf16[8,80,768]{2,1,0:T(8,128)(2,1)} %bitcast.149), calls=%async_computation.2 | async-start | bytes 1966080 | tf_op jit(solution)/shard_map/all_to_all | solution.py:161
  251.1 10.6 %copy-start.4 = (f32[2,8,40,3072]{3,2,1,0:T(8,128)}, f32[2,8,40,3072]{3,2,1,0:T(8,128)S(1)}, u32[]{:S(2)}) copy-start(f32[2,8,40,3072]{3,2,1,0:T(8,128)S(1)} %fusion.3) | copy-start | bytes 23592964
  269.5 28.3 %all-to-all-start.1 = ((bf16[8,80,768]{2,1,0:T(8,128)(2,1)}), bf16[8,80,768]{2,1,0:T(8,128)(2,1)S(1)}, u32[]{:S(2)}, u32[]{:S(2)}) async-start(bf16[8,80,768]{2,1,0:T(8,128)(2,1)} %bitcast.16), calls=%async_computation.1 | async-start | bytes 1966080 | tf_op jit(solution)/shard_map/all_to_all | solution.py:149
  284.6 8.5 %copy-start.66 = (bf16[8,2,40,3072]{3,2,0,1:T(8,128)(2,1)}, bf16[8,2,40,3072]{3,2,0,1:T(8,128)(2,1)S(1)}, u32[]{:S(2)}) copy-start(bf16[8,2,40,3072]{3,2,0,1:T(8,128)(2,1)S(1)} %fusion.15) | copy-start | bytes 11796484
  297.8 28.1 %all-to-all-start.3 = ((bf16[8,80,768]{2,1,0:T(8,128)(2,1)}), bf16[8,80,768]{2,1,0:T(8,128)(2,1)S(1)}, u32[]{:S(2)}, u32[]{:S(2)}) async-start(bf16[8,80,768]{2,1,0:T(8,128)(2,1)} %bitcast.150), calls=%async_computation.3 | async-start | bytes 1966080 | tf_op jit(solution)/shard_map/all_to_all | solution.py:172
  301.4 72.2 %reduce-scatter.20.cloned.1.call-start = ((), (), s32[]{:S(2)}) async-start(), calls=%async_computation.20 | async-start | bytes 1474560 | tf_op jit(solution)/shard_map/reduce_scatter | solution.py:264
  302.2 2.7 copy-start.54
  307.4 20.9 %copy-start.47 = (f32[512]{0:T(512)}, f32[512]{0:T(512)S(1)}, u32[]{:S(2)}) copy-start(f32[512]{0:T(512)S(1)} %mul.282) | copy-start | bytes 6148
  326.0 2.3 copy-start.28
  326.0 2.3 copy-start.37
  326.0 2.4 copy-start.40
  326.0 2.4 copy-start.43
  326.0 2.4 copy-start.57
  333.3 2.6 copy-start.31
  333.3 53.2 %reduce-scatter.18.cloned.1.call-start = ((), (), s32[]{:S(2)}) async-start(), calls=%async_computation.19 | async-start | bytes 1474560 | tf_op jit(solution)/shard_map/reduce_scatter | solution.py:261
  335.9 8.1 %copy-start.18 = (bf16[512,768]{1,0:T(8,128)(2,1)S(1)}, bf16[512,768]{1,0:T(8,128)(2,1)}, u32[]{:S(2)}) copy-start(bf16[512,768]{1,0:T(8,128)(2,1)} %param.18) | copy-start | bytes 2359300
  336.0 8.1 %copy-start.50 = (f32[512]{0:T(512)S(1)}, f32[512]{0:T(512)}, u32[]{:S(2)}) copy-start(f32[512]{0:T(512)} %copy-done.49) | copy-start | bytes 6148
  336.0 8.1 %copy-start.52 = (f32[768]{0:T(1024)S(1)}, f32[768]{0:T(1024)}, u32[]{:S(2)}) copy-start(f32[768]{0:T(1024)} %param.23) | copy-start | bytes 9220
  346.1 69.3 %reduce-scatter.14.cloned.1.call-start = ((), (), s32[]{:S(2)}) async-start(), calls=%async_computation.17 | async-start | bytes 1474560 | tf_op jit(solution)/shard_map/reduce_scatter | solution.py:255
  352.5 6.3 copy-start.6
  358.8 2.7 copy-start.3
  358.8 3.6 copy-start.19
  364.4 80.0 %reduce-scatter.16.cloned.1.call-start = ((), (), s32[]{:S(2)}) async-start(), calls=%async_computation.18 | async-start | bytes 1474560 | tf_op jit(solution)/shard_map/reduce_scatter | solution.py:258
  370.4 2.1 copy-start.48
  372.4 259.9 %reduce-scatter.22.cloned.1.call-start = ((), (), s32[]{:S(2)}) async-start(), calls=%async_computation.21 | async-start | bytes 245760
  373.6 281.6 %all-reduce.7.cloned.1.call-start = ((), (), s32[]{:S(2)}) async-start(), calls=%async_computation.22 | async-start | bytes 2359296 | tf_op jit(solution)/shard_map/psum | solution.py:248
  444.5 216.0 %reduce-scatter.12.cloned.1.call-start = ((), (), s32[]{:S(2)}) async-start(), calls=%async_computation.16 | async-start | bytes 11796480 | tf_op jit(solution)/shard_map/reduce_scatter | solution.py:188
  455.4 259.4 %reduce-scatter.10.cloned.1.call-start = ((), (), s32[]{:S(2)}) async-start(), calls=%async_computation.15 | async-start | bytes 11796480 | tf_op jit(solution)/shard_map/reduce_scatter | solution.py:185
  571.7 10.4 %copy-start.65 = (s32[1023]{0:T(1024)S(1)}, s32[1023]{0:T(1024)}, u32[]{:S(2)}) copy-start(s32[1023]{0:T(1024)} %param.22) | copy-start | bytes 12280
  571.7 10.9 %copy-start.25 = (bf16[12,64,512]{2,1,0:T(8,128)(2,1)S(1)}, bf16[12,64,512]{2,1,0:T(8,128)(2,1)}, u32[]{:S(2)}) copy-start(bf16[12,64,512]{2,1,0:T(8,128)(2,1)} %copy-done.24) | copy-start | bytes 2359300
  582.2 2.7 copy-start.33
  582.2 2.7 copy-start.63
  586.4 2.3 copy-start.53
  586.4 42.9 %copy-start.55 = (f32[512]{0:T(512)S(1)}, f32[512]{0:T(512)}, u32[]{:S(2)}) copy-start(f32[512]{0:T(512)} %get-tuple-element.28) | copy-start | bytes 6148
  655.1 3.7 copy-start.35
  655.1 4.6 copy-start.34
  660.5 58.5 %copy-start.1 = (f32[32,12]{0,1:T(8,128)S(1)}, f32[32,12]{0,1:T(8,128)}, u32[]{:S(2)}) copy-start(f32[32,12]{0,1:T(8,128)} %param.28) | copy-start | bytes 4612
  (19 other events, 28.3 us)
Sparse Core Ops, SparseCore 0:
  9.6 20.1 all-gather.7
  31.4 17.4 all-gather.9
  50.4 17.4 all-gather.5
  69.3 17.4 all-gather.11
  333.4 24.7 reduce-scatter.19
  360.8 25.7 reduce-scatter.17
  389.7 25.7 reduce-scatter.13
  418.7 25.7 reduce-scatter.15
  447.5 19.7 reduce-scatter.21
  471.0 80.9 all-reduce.6
  554.8 78.9 reduce-scatter.11
  636.4 78.4 reduce-scatter.9
where the time goes:
time: 735 us; the launch traced here: 726 us
  local copies, waits for them, and re-layouts  273 us (37%)
  waiting for transfers between devices  167 us (23%)
  matrix products  115 us (16%)
  other arithmetic  69.5 us (9%)
  blocking collectives  67.2 us (9%)
  starting transfers between devices  19.8 us (3%)
  between operations  15.5 us (2%)
    unnamed x143, local copies, waits for them, and re-layouts  113 us
    reduce_scatter x1, waiting for transfers between devices, body(): lax.psum_scatter(grad_w_in.astype(jnp.bfloat16), 'dp', scatter_dimension=...  49.7 us
    reshape x1, local copies, waits for them, and re-layouts, toeplitz_bias(): return window.reshape(head_count, length, 2 * length - 1)[:, :, :length]  49.2 us
    convert_element_type x1, local copies, waits for them, and re-layouts, diagonal_sums(): diag_sums = jnp.sum(sheared, axis=1, dtype=jnp.float32)[:, 1:width]  48.7 us
    psum x1, blocking collectives, body(): lax.psum((grad_gain_one, grad_gain_two, grad_rel), ('dp', 'expert'))  40.6 us
    reduce_scatter x1, waiting for transfers between devices, body(): lax.psum_scatter(summed[1].astype(jnp.bfloat16), 'dp', scatter_dimension=...  29.1 us
    reduce_scatter x1, waiting for transfers between devices, body(): lax.psum_scatter(summed[0].astype(jnp.bfloat16), 'dp', scatter_dimension=...  28.9 us
    slice x1, local copies, waits for them, and re-layouts, toeplitz_bias(): window = tiled[:, length - 1:length - 1 + length * (2 * length - 1)]  25.8 us
  transfers between devices with their start and end apart: 16, of which 8 were waited for; matrix products, arithmetic and copies ran while one was open for 59% of the time, Pallas kernels for 0%

commit v1 on v0

v1 whole, which is shorter than its diff:
```python
import math

import jax
import jax.numpy as jnp
from jax import lax
from jax.experimental import pallas as pl
from jax.experimental.pallas import tpu as pltpu
from jax.sharding import PartitionSpec as P

EPS = 1e-06
HIGH = lax.Precision.HIGHEST
F32 = jnp.float32
BF16 = jnp.bfloat16
VMEM_LIMIT = 56 * 1024 * 1024
TILE = 128
STRIP = 256
GELU_A = math.sqrt(2.0 / math.pi)
GELU_B = 0.044715


def dot(a, b):
    return jnp.dot(a, b, preferred_element_type=F32)


def dot_nt(a, b):
    return lax.dot_general(a, b, (((1,), (1,)), ((), ())), preferred_element_type=F32)


def params(**kw):
    return pltpu.CompilerParams(vmem_limit_bytes=VMEM_LIMIT, **kw)


def cost(flops, nbytes, trans=0):
    return pl.CostEstimate(flops=int(flops), bytes_accessed=int(nbytes), transcendentals=int(trans))


def rms_scale(stream):
    return lax.rsqrt(jnp.mean(stream * stream, axis=-1, keepdims=True) + EPS)


def norm_back(stream, gain, grad_out):
    scale = rms_scale(stream)
    grad_gain = jnp.sum(grad_out * (stream * scale), axis=0, keepdims=True)
    scaled = grad_out * gain
    inner = jnp.mean(scaled * stream, axis=-1, keepdims=True)
    grad_in = scale * scaled - stream * (scale * scale * scale * inner)
    return grad_in, grad_gain


def gelu_pair(v):
    sq = v * v
    inner = GELU_A * (v + GELU_B * (sq * v))
    th = jnp.tanh(inner)
    half = 0.5 * (1.0 + th)
    slope = half + (0.5 * v) * (1.0 - th * th) * (GELU_A + (3.0 * GELU_A * GELU_B) * sq)
    return v * half, slope


def place_kernel(target_ref, rows_ref, out_ref):
    slots, seq = out_ref.shape[0], rows_ref.shape[0]
    ids = lax.broadcasted_iota(jnp.int32, (slots, seq), 0)
    hot = (ids == target_ref[...]).astype(F32).astype(BF16)
    out_ref[...] = dot(hot, rows_ref[...]).astype(BF16)


def place(target_row, rows, slots):
    seq, width = rows.shape
    return pl.pallas_call(
        place_kernel,
        out_shape=jax.ShapeDtypeStruct((slots, width), BF16),
        compiler_params=params(),
        cost_estimate=cost(2 * slots * seq * width, 2 * (slots + seq) * width),
        name="place_cotangent",
    )(target_row, rows)


def bias_kernel(rel_ref, out_ref):
    heads, width = rel_ref.shape
    wide = out_ref.shape[2]
    for h in range(heads):
        base = jnp.broadcast_to(rel_ref[h : h + 1, :], (TILE, width))
        turned = pltpu.roll(base, width - (TILE - 1), 1, stride=1, stride_axis=0)
        out_ref[h] = turned[:, :wide]


def bias_tiles(rel_rev, seq):
    heads, width = rel_rev.shape
    wide = 2 * seq - TILE
    return pl.pallas_call(
        bias_kernel,
        out_shape=jax.ShapeDtypeStruct((heads, TILE, wide), F32),
        compiler_params=params(),
        cost_estimate=cost(heads * TILE * width, 4 * heads * TILE * wide),
        name="bias_tiles",
    )(rel_rev)


def attend_kernel(
    tok_ref, gain_ref, wq_ref, wk_ref, wv_ref, bias_ref, kseg_ref, qseg_ref,
    q_ref, k_ref, v_ref, kt_ref, e_ref, rinv_ref, ctxt_ref, normt_ref, normed_ref,
):
    seq = tok_ref.shape[0]
    heads = e_ref.shape[0]
    hd = q_ref.shape[1] // heads
    per_tile = TILE // hd

    @pl.when(pl.program_id(0) == 0)
    def _():
        stream = tok_ref[...].astype(F32)
        normed = stream * rms_scale(stream) * gain_ref[...]
        normed_ref[...] = normed.astype(BF16)
        normt_ref[...] = normed.T.astype(BF16)

    normed = normed_ref[...]
    q = (dot(normed, wq_ref[...]).astype(BF16).astype(F32) * (1.0 / math.sqrt(hd))).astype(BF16)
    k32 = dot(normed, wk_ref[...])
    v32 = dot(normed, wv_ref[...])
    q_ref[...] = q
    k_ref[...] = k32.astype(BF16)
    v_ref[...] = v32.astype(BF16)
    kt_ref[...] = k32.T.astype(BF16)
    vt = v32.T.astype(BF16)
    lane = lax.broadcasted_iota(jnp.int32, (seq, TILE), 1) // hd
    kseg = kseg_ref[...]
    qseg = qseg_ref[...]
    for h in range(heads):
        tile = h // per_tile
        k_pair = k_ref[:, tile * TILE : (tile + 1) * TILE]
        q_pair = q_ref[:, tile * TILE : (tile + 1) * TILE]
        q_own = jnp.where(lane == h % per_tile, q_pair, jnp.zeros_like(q_pair))
        k_all = jnp.concatenate([k_pair, kseg], axis=1)
        q_all = jnp.concatenate([q_own, qseg], axis=1)
        for start in range(0, seq, STRIP):
            scores = dot_nt(k_all, q_all[start : start + STRIP])
            parts = []
            for b in range(0, seq, TILE):
                off = seq - TILE - b + start
                parts.append(scores[b : b + TILE] + bias_ref[h, :, off : off + STRIP])
            scores = jnp.concatenate(parts, axis=0)
            e = jnp.exp(scores - jnp.max(scores, axis=0, keepdims=True))
            rinv = 1.0 / jnp.sum(e, axis=0, keepdims=True)
            eb = e.astype(BF16)
            e_ref[h, :, start : start + STRIP] = eb
            rinv_ref[h, :, start : start + STRIP] = rinv
            ctxt = dot(vt[h * hd : (h + 1) * hd], eb) * rinv
            ctxt_ref[h * hd : (h + 1) * hd, start : start + STRIP] = ctxt.astype(BF16)


def attend(tokens, gain, w_qkv, bias, kseg, qseg, heads, group):
    seq, width = tokens.shape
    cols = width // heads * group
    steps = heads // group
    wide = bias.shape[2]
    whole = lambda a: pl.BlockSpec(a.shape, lambda g: (0,) * a.ndim)
    col = lambda base: pl.BlockSpec((width, cols), lambda g: (0, base * steps + g))
    nat = pl.BlockSpec((seq, cols), lambda g: (0, g))
    tr = pl.BlockSpec((cols, seq), lambda g: (g, 0))
    sds = jax.ShapeDtypeStruct
    return pl.pallas_call(
        attend_kernel,
        grid=(steps,),
        in_specs=[
            whole(tokens), whole(gain), col(0), col(1), col(2),
            pl.BlockSpec((group, TILE, wide), lambda g: (g, 0, 0)), whole(kseg), whole(qseg),
        ],
        out_specs=[
            nat, nat, nat, tr,
            pl.BlockSpec((group, seq, seq), lambda g: (g, 0, 0)),
            pl.BlockSpec((group, 1, seq), lambda g: (g, 0, 0)),
            tr,
            pl.BlockSpec((width, seq), lambda g: (0, 0)),
        ],
        out_shape=[
            sds((seq, width), BF16), sds((seq, width), BF16), sds((seq, width), BF16),
            sds((width, seq), BF16), sds((heads, seq, seq), BF16), sds((heads, 1, seq), F32),
            sds((width, seq), BF16), sds((width, seq), BF16),
        ],
        scratch_shapes=[pltpu.VMEM((seq, width), BF16)],
        compiler_params=params(dimension_semantics=("arbitrary",)),
        cost_estimate=cost(
            6 * seq * width * width + 4 * seq * seq * width,
            2 * (3 * width * width + 9 * seq * width + heads * seq * seq) + 4 * bias.size,
            heads * seq * seq,
        ),
        name="attention_forward",
    )(tokens, gain, w_qkv, w_qkv, w_qkv, bias, kseg, qseg)


def middle_kernel(tok_ref, ctxt_ref, wo_ref, gain_ref, target_ref, middle_ref, placed_ref):
    seq = tok_ref.shape[0]
    context = ctxt_ref[...].astype(F32).T.astype(BF16)
    middle = tok_ref[...].astype(F32) + dot(context, wo_ref[...])
    middle_ref[...] = middle
    normed = (middle * rms_scale(middle) * gain_ref[...]).astype(BF16)
    slots = placed_ref.shape[0]
    ids = lax.broadcasted_iota(jnp.int32, (slots, seq), 0)
    hot = (ids == target_ref[...]).astype(F32).astype(BF16)
    placed_ref[...] = dot(hot, normed).astype(BF16)


def middle_step(tokens, ctxt, w_out, gain, target_row, slots):
    seq, width = tokens.shape
    return pl.pallas_call(
        middle_kernel,
        out_shape=[
            jax.ShapeDtypeStruct((seq, width), F32),
            jax.ShapeDtypeStruct((slots, width), BF16),
        ],
        compiler_params=params(),
        cost_estimate=cost(
            2 * seq * width * width + 2 * slots * seq * width,
            2 * width * width + 8 * seq * width + 2 * slots * width,
        ),
        name="output_projection_dispatch",
    )(tokens, ctxt, w_out, gain, target_row)


def gate_of(logits, expert):
    top = jnp.max(logits, axis=-1, keepdims=True)
    ex = jnp.exp(logits - top)
    prob = ex / jnp.sum(ex, axis=-1, keepdims=True)
    hot = lax.broadcasted_iota(jnp.int32, logits.shape, 1) == expert
    gate = jnp.sum(jnp.where(hot, prob, 0.0), axis=-1, keepdims=True)
    return prob, hot, gate


def expert_kernel(
    num_ref, x_ref, c_ref, wr_ref, win_ref, wout_ref,
    scaled_ref, grad_ref, router_ref, gp_ref, acc_p, acc_g,
):
    step = pl.program_id(0)

    @pl.when(step == 0)
    def _():
        _, _, gate = gate_of(dot(x_ref[...], wr_ref[...]), num_ref[0])
        gp_ref[...] = (gate * c_ref[...].astype(F32)).astype(BF16)
        acc_p[...] = jnp.zeros_like(acc_p)
        acc_g[...] = jnp.zeros_like(acc_g)

    pre = dot(x_ref[...], win_ref[0])
    hidden, slope = gelu_pair(pre)
    acc_p[...] += dot(hidden.astype(BF16), wout_ref[0])
    grad_hidden = dot_nt(gp_ref[...], wout_ref[0])
    acc_g[...] += dot_nt((grad_hidden * slope).astype(BF16), win_ref[0])

    @pl.when(step == pl.num_programs(0) - 1)
    def _():
        x = x_ref[...]
        prob, hot, gate = gate_of(dot(x, wr_ref[...]), num_ref[0])
        produced = acc_p[...]
        scaled_ref[...] = (gate * produced).astype(BF16)
        grad_gate = jnp.sum(
            c_ref[...].astype(F32) * produced.astype(BF16).astype(F32), axis=-1, keepdims=True
        )
        grad_logits = prob * (jnp.where(hot, grad_gate, 0.0) - gate * grad_gate)
        logits_b = grad_logits.astype(BF16)
        grad_ref[...] = (acc_g[...] + dot_nt(logits_b, wr_ref[...])).astype(BF16)
        router_ref[...] = dot(grad_logits.T.astype(BF16), x)


def expert_step(number, x, c, w_router, w_in, w_out, local, block):
    rows, width = x.shape
    ff = w_in.shape[2]
    experts = w_router.shape[1]
    whole = lambda a: pl.BlockSpec(a.shape, lambda f: (0,) * a.ndim)
    row_spec = pl.BlockSpec((rows, width), lambda f: (0, 0))
    return pl.pallas_call(
        expert_kernel,
        grid=(ff // block,),
        in_specs=[
            pl.BlockSpec(memory_space=pltpu.SMEM),
            whole(x),
            pl.BlockSpec((rows, width), lambda f: (local, 0)),
            whole(w_router),
            pl.BlockSpec((1, width, block), lambda f: (local, 0, f)),
            pl.BlockSpec((1, block, width), lambda f: (local, f, 0)),
        ],
        out_specs=[row_spec, row_spec, pl.BlockSpec((experts, width), lambda f: (0, 0))],
        out_shape=[
            jax.ShapeDtypeStruct((rows, width), BF16),
            jax.ShapeDtypeStruct((rows, width), BF16),
            jax.ShapeDtypeStruct((experts, width), F32),
        ],
        scratch_shapes=[
            pltpu.VMEM((rows, width), BF16),
            pltpu.VMEM((rows, width), F32),
            pltpu.VMEM((rows, width), F32),
        ],
        compiler_params=params(dimension_semantics=("arbitrary",)),
        cost_estimate=cost(
            8 * rows * width * ff, 4 * width * ff + 8 * rows * width, rows * ff
        ),
        name="expert_rows",
    )(number, x, c, w_router, w_in, w_out)


def expert_grad_kernel(
    num_ref, x_ref, c_ref, wr_ref, win_ref, wout_ref, gin_ref, gout_ref, gp_ref, xt_ref
):
    parts, rows, width = x_ref.shape
    x = x_ref[...].reshape(parts * rows, width)

    @pl.when(pl.program_id(0) == 0)
    def _():
        _, _, gate = gate_of(dot(x, wr_ref[...]), num_ref[1])
        c = c_ref[...].reshape(parts * rows, width)
        gp_ref[...] = (gate * c.astype(F32)).astype(BF16)
        xt_ref[...] = x.astype(F32).T.astype(BF16)

    gp = gp_ref[...]
    pre_t = dot_nt(win_ref[0].astype(F32).T.astype(BF16), x)
    hidden_t, slope_t = gelu_pair(pre_t)
    grad_hidden_t = dot_nt(wout_ref[0], gp)
    gout_ref[0] = dot(hidden_t.astype(BF16), gp)
    gin_ref[0] = dot_nt(xt_ref[...], (grad_hidden_t * slope_t).astype(BF16))


def expert_grads(numbers, x_all, c_all, w_router, w_in, w_out, local, n_dp):
    parts, rows, width = x_all.shape
    ff = w_in.shape[2]
    part = ff // n_dp
    block = 256 if part % 256 == 0 else 128
    steps = part // block
    whole = lambda a: pl.BlockSpec(a.shape, lambda f, n: (0,) * a.ndim)
    return pl.pallas_call(
        expert_grad_kernel,
        grid_spec=pltpu.PrefetchScalarGridSpec(
            num_scalar_prefetch=1,
            grid=(steps,),
            in_specs=[
                whole(x_all),
                pl.BlockSpec((parts, rows, width), lambda f, n: (0, local, 0)),
                whole(w_router),
                pl.BlockSpec((1, width, block), lambda f, n: (local, 0, n[0] * steps + f)),
                pl.BlockSpec((1, block, width), lambda f, n: (local, n[0] * steps + f, 0)),
            ],
            out_specs=[
                pl.BlockSpec((1, width, block), lambda f, n: (0, 0, f)),
                pl.BlockSpec((1, block, width), lambda f, n: (0, f, 0)),
            ],
            scratch_shapes=[
                pltpu.VMEM((parts * rows, width), BF16),
                pltpu.VMEM((width, parts * rows), BF16),
            ],
        ),
        out_shape=[
            jax.ShapeDtypeStruct((1, width, part), F32),
            jax.ShapeDtypeStruct((1, part, width), F32),
        ],
        compiler_params=params(dimension_semantics=("arbitrary",)),
        cost_estimate=cost(
            8 * parts * rows * width * part,
            4 * parts * rows * width + 12 * width * part,
            parts * rows * part,
        ),
        name="expert_weight_grads",
    )(numbers, x_all, c_all, w_router, w_in, w_out)


def middle_back_kernel(
    *refs,
):
    (cot_ref, middle_ref, gain_ref, target_ref, ctxt_ref, wo_ref), refs = refs[:6], refs[6:]
    back_refs, (gmid_ref, gctx_ref, gwo_ref, ggain_ref) = refs[:-4], refs[-4:]
    seq, width = cot_ref.shape
    target = target_ref[...]
    grad = jnp.zeros((seq, width), F32)
    for l, back in enumerate(back_refs):
        rows = back.shape[0]
        ids = lax.broadcasted_iota(jnp.int32, (seq, rows), 1) + l * rows
        hot = (ids == target).astype(F32).astype(BF16)
        grad = grad + dot(hot, back[...])
    grad_in, grad_gain = norm_back(middle_ref[...], gain_ref[...], grad)
    ggain_ref[...] = grad_gain
    grad_middle = cot_ref[...].astype(F32) + grad_in
    gmid_ref[...] = grad_middle
    grad_attn = grad_middle.astype(BF16)
    gctx_ref[...] = dot_nt(grad_attn, wo_ref[...]).astype(BF16)
    gwo_ref[...] = dot(ctxt_ref[...], grad_attn).astype(BF16)


def middle_back(cot, middle, gain, target_col, ctxt, w_out, backs):
    seq, width = cot.shape
    sds = jax.ShapeDtypeStruct
    slots = sum(b.shape[0] for b in backs)
    return pl.pallas_call(
        middle_back_kernel,
        out_shape=[
            sds((seq, width), F32), sds((seq, width), BF16), sds((width, width), BF16),
            sds((1, width), F32),
        ],
        compiler_params=params(),
        cost_estimate=cost(
            4 * seq * width * width + 2 * slots * seq * width,
            4 * width * width + 14 * seq * width + 2 * slots * width,
        ),
        name="second_norm_backward",
    )(cot, middle, gain, target_col, ctxt, w_out, *backs)


def attend_back_kernel(
    tok_ref, gain_ref, gmid_ref, normt_ref, q_ref, k_ref, v_ref, kt_ref, e_ref, rinv_ref, do_ref,
    wq_ref, wk_ref, wv_ref,
    gq_ref, gk_ref, gv_ref, diag_ref, gtok_ref, ggain_ref, sum_ref, acc_ref,
):
    seq = tok_ref.shape[0]
    heads = e_ref.shape[0]
    cols = q_ref.shape[1]
    hd = cols // heads
    per_tile = TILE // hd
    step = pl.program_id(0)
    lane = lax.broadcasted_iota(jnp.int32, (seq, TILE), 1) // hd
    row_bit = lax.broadcasted_iota(jnp.int32, (8, 2 * seq), 0)
    dk_tiles, dv_tiles, dqt_rows = [], [], []
    for h in range(heads):
        tile = h // per_tile
        sl = slice(tile * TILE, (tile + 1) * TILE)
        zero = jnp.zeros((seq, TILE), BF16)
        q_own = jnp.where(lane == h % per_tile, q_ref[:, sl], zero)
        do_own = jnp.where(lane == h % per_tile, do_ref[:, sl], zero)
        v_pair = v_ref[:, sl]
        acc_ref[...] = jnp.zeros_like(acc_ref)
        dk = jnp.zeros((seq, TILE), F32)
        dv = jnp.zeros((seq, TILE), F32)
        dqt_parts = []
        for start in range(0, seq, STRIP):
            st = slice(start, start + STRIP)
            p = e_ref[h, :, st].astype(F32) * rinv_ref[h, :, st]
            t = dot_nt(v_pair, do_own[st]) * p
            ds = t - p * jnp.sum(t, axis=0, keepdims=True)
            dsb = ds.astype(BF16)
            dv = dv + dot(p.astype(BF16), do_own[st])
            dk = dk + dot(dsb, q_own[st])
            dqt_parts.append(dot(kt_ref[h * hd : (h + 1) * hd, :], dsb))
            for b in range(0, seq, TILE):
                off = seq - TILE - b + start
                acc_ref[:, off : off + STRIP] += ds[b : b + TILE]
        if h % per_tile == 0:
            dk_tiles.append(dk)
            dv_tiles.append(dv)
        else:
            dk_tiles[-1] = dk_tiles[-1] + dk
            dv_tiles[-1] = dv_tiles[-1] + dv
        dqt_rows.append(jnp.concatenate(dqt_parts, axis=1))
        folded = acc_ref[...]
        half = TILE // 2
        while half >= 8:
            folded = folded[:half] + pltpu.roll(folded[half:], 2 * seq - half, 1)
            half //= 2
        for bit in (4, 2, 1):
            turned = pltpu.roll(folded, 2 * seq - bit, 1)
            folded = jnp.where((row_bit & bit) != 0, turned, folded)
        diag_ref[h] = jnp.sum(folded, axis=0, keepdims=True)
    dqt = (jnp.concatenate(dqt_rows, axis=0) * (1.0 / math.sqrt(hd))).astype(BF16)
    dq = dqt.astype(F32).T.astype(BF16)
    dk = jnp.concatenate(dk_tiles, axis=1).astype(BF16)
    dv = jnp.concatenate(dv_tiles, axis=1).astype(BF16)
    normt = normt_ref[...]
    gq_ref[...] = dot(normt, dq).astype(BF16)
    gk_ref[...] = dot(normt, dk).astype(BF16)
    gv_ref[...] = dot(normt, dv).astype(BF16)
    grad = dot_nt(dq, wq_ref[...]) + dot_nt(dk, wk_ref[...]) + dot_nt(dv, wv_ref[...])

    @pl.when(step == 0)
    def _():
        sum_ref[...] = grad

    @pl.when(step > 0)
    def _():
        sum_ref[...] += grad

    @pl.when(step == pl.num_programs(0) - 1)
    def _():
        stream = tok_ref[...].astype(F32)
        grad_in, grad_gain = norm_back(stream, gain_ref[...], sum_ref[...])
        gtok_ref[...] = gmid_ref[...] + grad_in
        ggain_ref[...] = grad_gain


def attend_back(tokens, gain, grad_middle, normt, q, k, v, kt, e, rinv, grad_ctx, w_qkv, group):
    seq, width = tokens.shape
    heads = e.shape[0]
    cols = width // heads * group
    steps = heads // group
    whole = lambda a: pl.BlockSpec(a.shape, lambda g: (0,) * a.ndim)
    col = lambda base: pl.BlockSpec((width, cols), lambda g: (0, base * steps + g))
    nat = pl.BlockSpec((seq, cols), lambda g: (0, g))
    tr = pl.BlockSpec((cols, seq), lambda g: (g, 0))
    gcol = pl.BlockSpec((width, cols), lambda g: (0, g))
    sds = jax.ShapeDtypeStruct
    return pl.pallas_call(
        attend_back_kernel,
        grid=(steps,),
        in_specs=[
            whole(tokens), whole(gain), whole(grad_middle), whole(normt), nat, nat, nat, tr,
            pl.BlockSpec((group, seq, seq), lambda g: (g, 0, 0)),
            pl.BlockSpec((group, 1, seq), lambda g: (g, 0, 0)),
            nat, col(0), col(1), col(2),
        ],
        out_specs=[
            gcol, gcol, gcol,
            pl.BlockSpec((group, 1, 2 * seq), lambda g: (g, 0, 0)),
            pl.BlockSpec((seq, width), lambda g: (0, 0)),
            pl.BlockSpec((1, width), lambda g: (0, 0)),
        ],
        out_shape=[
            sds((width, width), BF16), sds((width, width), BF16), sds((width, width), BF16),
            sds((heads, 1, 2 * seq), F32), sds((seq, width), F32), sds((1, width), F32),
        ],
        scratch_shapes=[pltpu.VMEM((seq, width), F32), pltpu.VMEM((TILE, 2 * seq), F32)],
        compiler_params=params(dimension_semantics=("arbitrary",)),
        cost_estimate=cost(
            12 * seq * width * width + 8 * seq * seq * width,
            2 * (6 * width * width + 8 * seq * width + heads * seq * seq) + 8 * seq * width,
        ),
        name="attention_backward",
    )(tokens, gain, grad_middle, normt, q, k, v, kt, e, rinv, grad_ctx, w_qkv, w_qkv, w_qkv)


def output_kernel(middle_ref, target_ref, *refs):
    out_ref = refs[-1]
    seq = middle_ref.shape[0]
    total = middle_ref[...]
    for l, back in enumerate(refs[:-1]):
        rows = back.shape[0]
        ids = lax.broadcasted_iota(jnp.int32, (seq, rows), 1) + l * rows
        hot = (ids == target_ref[...]).astype(F32).astype(BF16)
        total = total + dot(hot, back[...])
    out_ref[...] = total.astype(BF16)


def output_step(middle, target_col, backs):
    seq, width = middle.shape
    slots = sum(b.shape[0] for b in backs)
    return pl.pallas_call(
        output_kernel,
        out_shape=jax.ShapeDtypeStruct((seq, width), BF16),
        compiler_params=params(),
        cost_estimate=cost(2 * slots * seq * width, 6 * seq * width + 2 * slots * width),
        name="layer_output",
    )(middle, target_col, *backs)


def butterfly_sum(value, axes):
    for axis in axes:
        size = lax.axis_size(axis)
        if size & (size - 1):
            value = lax.psum(value, axis)
            continue
        bit = 1
        while bit < size:
            value = value + lax.ppermute(value, axis, [(i, i ^ bit) for i in range(size)])
            bit *= 2
    return value


def body(
    tokens, segments, routes, slots, bucket_table, gain_attn, w_query, w_key, w_value, w_output,
    rel_bias, gain_ffn, w_router, w_in, w_out, cotangent,
):
    seq, width = tokens.shape
    buckets, heads = rel_bias.shape
    experts = w_router.shape[1]
    n_dp = lax.axis_size("dp")
    peers = lax.axis_size("expert")
    local = w_in.shape[0]
    capacity = max(2, (5 * seq + 4 * experts - 1) // (4 * experts))
    rows = peers * capacity
    dp_index = lax.axis_index("dp")
    expert_index = lax.axis_index("expert")

    w_qkv = lax.all_gather(
        jnp.concatenate([w_query, w_key, w_value], axis=1), "dp", axis=0, tiled=True
    )
    full_o = lax.all_gather(w_output, "dp", axis=0, tiled=True)
    full_r = lax.all_gather(w_router, "dp", axis=0, tiled=True)

    order = (routes % local) * rows + (routes // local) * capacity + slots
    target = jnp.where(slots >= 0, order, -1)
    target_row = target[None, :]
    target_col = target[:, None]
    gain_one = gain_attn[None, :]
    gain_two = gain_ffn[None, :]

    def exchange(values):
        parts = values.reshape(peers, capacity, width)
        return lax.all_to_all(parts, "expert", split_axis=0, concat_axis=0, tiled=True).reshape(
            rows, width
        )

    c_placed = place(target_row, cotangent, local * rows)
    c_here = jnp.concatenate(
        [exchange(c_placed[l * rows : (l + 1) * rows]) for l in range(local)], axis=0
    )
    c_all = lax.all_gather(c_here, "dp", axis=0, tiled=False)

    span = 2 * seq
    reversed_table = jnp.concatenate([bucket_table[::-1], jnp.full((1,), -1, jnp.int32)])
    bucket_ids = jnp.arange(buckets, dtype=jnp.int32)
    hot_rev = (bucket_ids[:, None] == reversed_table[None, :]).astype(F32)
    rel_rev = jnp.dot(rel_bias.T, hot_rev, precision=HIGH)
    shifted = jnp.roll(reversed_table, 1 - TILE)
    hot_shifted = (shifted[:, None] == bucket_ids[None, :]).astype(F32)
    bias = bias_tiles(rel_rev, seq)
    marks = jnp.arange(TILE, dtype=jnp.int32)[None, :]
    same = segments[0][:, None] == marks
    kseg = same.astype(BF16)
    qseg = jnp.where(same, 0.0, -1e9).astype(BF16)

    q, k, v, kt, e, rinv, ctxt, normt = attend(
        tokens, gain_one, w_qkv, bias, kseg, qseg, heads, 4
    )
    middle, placed = middle_step(tokens, ctxt, full_o, gain_two, target_row, local * rows)

    backs, returns, router_terms, gin, gout = [], [], [], [], []
    for l in range(local):
        x = exchange(placed[l * rows : (l + 1) * rows])
        number = jnp.reshape(expert_index * local + l, (1,)).astype(jnp.int32)
        scaled, grad_x, router_term = expert_step(
            number, x, c_here, full_r, w_in, w_out, l, 512
        )
        backs.append(exchange(grad_x))
        returns.append(exchange(scaled))
        router_terms.append(router_term)
        numbers = jnp.stack([dp_index, expert_index * local + l]).astype(jnp.int32)
        x_all = lax.all_gather(x, "dp", axis=0, tiled=False)
        gi, go = expert_grads(numbers, x_all, c_all, full_r, w_in, w_out, l, n_dp)
        gin.append(gi)
        gout.append(go)
    grad_w_in = jnp.concatenate(gin, axis=0)
    grad_w_out = jnp.concatenate(gout, axis=0)

    grad_middle, grad_ctx, gw_o, ggain_two = middle_back(
        cotangent, middle, gain_two, target_col, ctxt, full_o, backs
    )
    gw_q, gw_k, gw_v, diag, grad_tokens, ggain_one = attend_back(
        tokens, gain_one, grad_middle, normt, q, k, v, kt, e, rinv, grad_ctx, w_qkv, 4
    )
    output = output_step(middle, target_col, returns)

    def reduce_dense(term):
        part = lax.psum_scatter(term, "dp", scatter_dimension=0, tiled=True)
        return lax.psum(part, "expert").astype(F32)

    shard_o = reduce_dense(gw_o)
    shard_qkv = reduce_dense(jnp.concatenate([gw_q, gw_k, gw_v], axis=1))

    grad_rel = jnp.dot(diag.reshape(heads, span), hot_shifted, precision=HIGH)
    early = butterfly_sum(
        jnp.concatenate([sum(router_terms), ggain_two], axis=0), ("dp", "expert")
    )
    rel_row = jnp.pad(grad_rel.reshape(1, heads * buckets), ((0, 0), (0, width - heads * buckets)))
    late = butterfly_sum(jnp.concatenate([ggain_one, rel_row], axis=0), ("dp", "expert"))
    shard_rows = width // n_dp
    grad_router = lax.dynamic_slice_in_dim(early[:experts], dp_index * shard_rows, shard_rows, 1).T
    total_rel = late[1, : heads * buckets].reshape(heads, buckets).T
    return (
        output,
        grad_tokens,
        late[0],
        shard_qkv[:, :width],
        shard_qkv[:, width : 2 * width],
        shard_qkv[:, 2 * width :],
        shard_o,
        total_rel,
        early[experts],
        grad_router,
        grad_w_in,
        grad_w_out,
    )


def solution(mesh):
    in_specs = (
        P(("dp", "expert"), None),
        P(("dp", "expert"), None),
        P(("dp", "expert")),
        P(("dp", "expert")),
        P(),
        P(),
        P("dp", None),
        P("dp", None),
        P("dp", None),
        P("dp", None),
        P(),
        P(),
        P("dp", None),
        P("expert", None, None),
        P("expert", None, None),
        P(("dp", "expert"), None),
    )
    out_specs = (
        P(("dp", "expert"), None),
        P(("dp", "expert"), None),
        P(),
        P("dp", None),
        P("dp", None),
        P("dp", None),
        P("dp", None),
        P(),
        P(),
        P("dp", None),
        P("expert", None, "dp"),
        P("expert", "dp", None),
    )
    return jax.shard_map(body, mesh=mesh, in_specs=in_specs, out_specs=out_specs, check_vma=False)
```

time: 735 us -> 406 us (0.55); the launches traced: 726 us -> 405 us
  local copies, waits for them, and re-layouts: 273 us -> 14.1 us
  matrix products: 115 us -> 1.18 us
  Pallas kernels: 0 us -> 112 us
  other arithmetic: 69.5 us -> 18.3 us
  blocking collectives: 67.2 us -> 24.8 us
  starting transfers between devices: 19.8 us -> 44.1 us
  waiting for transfers between devices: 167 us -> 177 us
    reduce_scatter x6 -> x2, waiting for transfers between devices: 121 us -> 0.01 us  [reduce_dense(): part = lax.psum_scatter(term, 'dp', scatter_dimension=0, tiled=True)]
    dot_general x29 -> x2, matrix products: 115 us -> 1.18 us  [the longest x1 0.8 us: body(): rel_rev = jnp.dot(rel_bias.T, hot_rev, precision=HIGH)]
    pallas_call x0 -> x11, Pallas kernels: none -> 112 us  [the longest x2 26.7 us: expert_step(): pl.pallas_call(expert_kernel, grid=(ff // block,), in_specs=[pl.BlockSpec...]
    unnamed x143 -> x48, local copies, waits for them, and re-layouts: 113 us -> 1.81 us
    psum x1, waiting for transfers between devices: 0.01 us -> 63.3 us  [reduce_dense(): return lax.psum(part, 'expert').astype(F32)]
    psum x2 -> x0, blocking collectives: 62 us -> none  [the longest x1 40.6 us: body(): lax.psum((grad_gain_one, grad_gain_two, grad_rel), ('dp', 'expert'))]
    all_gather x4 -> x5, waiting for transfers between devices: 0.03 us -> 58 us  [the longest x2 34.4 us: body(): x_all = lax.all_gather(x, 'dp', axis=0, tiled=False)]
    convert_element_type x7 -> x0, local copies, waits for them, and re-layouts: 51.8 us -> none  [the longest x1 48.7 us: diagonal_sums(): diag_sums = jnp.sum(sheared, axis=1, dtype=jnp.float32)[:, 1:width]]
  transfers between devices with their start and end apart: 16 -> 25, of which waited for: 8 -> 14; matrix products, arithmetic and copies ran while one was open for 59% -> 7% of each run, Pallas kernels for 0% -> 26%
where the time goes in v1:
time: 406 us; the launch traced here: 405 us
  waiting for transfers between devices  177 us (44%)
  Pallas kernels  112 us (28%)
  starting transfers between devices  44.1 us (11%)
  blocking collectives  24.8 us (6%)
  other arithmetic  18.3 us (5%)
  between operations  14.5 us (4%)
  local copies, waits for them, and re-layouts  14.1 us (3%)
    psum x1, waiting for transfers between devices, reduce_dense(): return lax.psum(part, 'expert').astype(F32)  63.3 us
    all_to_all x7, waiting for transfers between devices, exchange(): lax.all_to_all(parts, 'expert', split_axis=0, concat_axis=0, tiled=True)  39.5 us
    all_gather x2, waiting for transfers between devices, body(): x_all = lax.all_gather(x, 'dp', axis=0, tiled=False)  34.4 us
    all_to_all x7, starting transfers between devices, exchange(): lax.all_to_all(parts, 'expert', split_axis=0, concat_axis=0, tiled=True)  32.9 us
    pallas_call x2, Pallas kernels, expert_step(): pl.pallas_call(expert_kernel, grid=(ff // block,), in_specs=[pl.BlockSpec...  26.7 us
    pallas_call x2, Pallas kernels, expert_grads(): pl.pallas_call(expert_grad_kernel, grid_spec=pltpu.PrefetchScalarGridSpec...  26.1 us
    all_gather x1, waiting for transfers between devices, body(): c_all = lax.all_gather(c_here, 'dp', axis=0, tiled=False)  23.2 us
    pallas_call x1, Pallas kernels, attend_back(): pl.pallas_call(attend_back_kernel, grid=(steps,), in_specs=[whole(tokens)...  21.5 us
  transfers between devices with their start and end apart: 25, of which 14 were waited for; matrix products, arithmetic and copies ran while one was open for 7% of the time, Pallas kernels for 26%

profile of v1, /device:TPU:0, one launch (start us, length us, event | category | flops | bytes accessed | tf_op | source)
XLA Modules:
  0.0 405.3 jit_solution(16945182224766124963)
XLA Ops:
  7.3 2.1 pad_maximum_fusion.4
  9.4 0.7 all-gather.10.cloned.1.call-update
  10.2 0.6 fusion.10
  10.8 2.8 place_cotangent.1
  13.6 2.2 fusion.17
  15.8 7.3 %all-to-all-start.2 = ((bf16[8,40,768]{2,1,0:T(8,128)(2,1)}), bf16[8,40,768]{2,1,0:T(8,128)(2,1)S(1)}, u32[]{:S(2)}, u32[]{:S(2)}) async-start(bf16[8,40,768]{2,1,0:T(8,128)(2,1)} %bitcast.9), calls=%async_computation.2 | async-start | bytes 983040 | tf_op jit(solution)/shard_map/all_to_all | solution.py:587
  23.3 0.8 fusion.2.kseg_ref
  24.1 12.8 %all-to-all-done.2 = bf16[8,40,768]{2,1,0:T(8,128)(2,1)S(1)} async-done(((bf16[8,40,768]{2,1,0:T(8,128)(2,1)}), bf16[8,40,768]{2,1,0:T(8,128)(2,1)S(1)}, u32[]{:S(2)}, u32[]{:S(2)}) %all-to-all-start.2) | async-done | bytes 491552 | tf_op jit(solution)/shard_map/all_to_all | solution.py:587
  36.8 3.6 all-to-all-start.1
  40.5 0.8 convolution_bitcast_fusion.rel_ref
  41.3 0.6 broadcast_in_dim.27.gain_ref
  41.8 0.6 broadcast_in_dim.30.gain_ref.refs_2_
  42.4 4.9 %bias_tiles.1.bias_ref = f32[12,128,896]{2,1,0:T(8,128)} custom-call(f32[12,1024]{1,0:T(8,128)} %convolution_bitcast_fusion.rel_ref), custom_call_target="tpu_custom_call" | custom-call | flops 1572864 | bytes 5505024 | tf_op jit(solution)/shard_map/bias_tiles/pallas_call | solution.py:89
  47.3 0.8 select_convert_fusion.qseg_ref
  48.1 14.3 %attention_forward.1 = (bf16[512,768]{1,0:T(8,128)(2,1)}, bf16[512,768]{1,0:T(8,128)(2,1)}, bf16[512,768]{1,0:T(8,128)(2,1)}, bf16[768,512]{1,0:T(8,128)(2,1)}, ...) custom-call(bf16[512,768]{1,0:T(8,128)(2,1)} %tok_ref.5, ...), custom_call_target="tpu_custom_call" | custom-call | flops 2617245696 | bytes 22413312 | tf_op jit(solution)/shard_map/attention_forward/pallas_call | solution.py:159
  62.7 4.5 %output_projection_dispatch.1 = (f32[512,768]{1,0:T(8,128)}, bf16[640,768]{1,0:T(8,128)(2,1)}) custom-call(bf16[512,768]{1,0:T(8,128)(2,1)} %tok_ref.5, bf16[768,512]{1,0:T(8,128)(2,1)} %get-tuple-element.42.ctxt_ref.refs_4_, bf16[768,768]{1,0:T(8,128)(2,1)} %all-gather.10.cloned.1.call-done.wo_ref.refs_5_, f32[1,768]{1,0:T(1,128)} %broadcast_in_dim.30.gain_ref.refs_2_, ...), custom_call_target="tpu_custom_call" | custom-call | flops 1107296256 | bytes 5308416 | tf_op jit(solution)/shard_map/output_projection_dispatch/pallas_call | solution.py:203
  67.3 2.0 fusion.16
  69.3 19.6 %all_to_all.40 = bf16[8,40,768]{2,1,0:T(8,128)(2,1)} all-to-all(bf16[8,40,768]{2,1,0:T(8,128)(2,1)S(1)} %bitcast.47), channel_id=1, replica_groups=mesh['dp'=4,'expert'=8] {'expert'}, dimensions={0} | all-to-all | bytes 983040 | tf_op jit(solution)/shard_map/all_to_all | solution.py:587
  88.9 3.6 all-to-all-start.4
  92.6 5.2 %all-gather.1 = bf16[4,192,16]{1,2,0:T(8,128)(2,1)S(1)} all-gather(bf16[1,192,16]{1,2,0:T(8,128)(2,1)S(1)} %bitcast.61), channel_id=1, replica_groups=mesh['dp'=4,'expert'=8] {'dp'}, dimensions={0}, use_global_device_ids=true | all-gather | bytes 30720 | tf_op jit(solution)/shard_map/all_gather | solution.py:576
  97.7 0.8 copy.32
  98.6 1.1 pad_maximum_fusion.3.c_ref
  99.6 13.3 %expert_rows.2 = (bf16[320,768]{1,0:T(8,128)(2,1)}, bf16[320,768]{1,0:T(8,128)(2,1)}, f32[16,768]{1,0:T(8,128)}) custom-call(s32[1]{0:T(128)} %bitcast.4.num_ref, bf16[320,768]{1,0:T(8,128)(2,1)} %bitcast.41, bf16[640,768]{1,0:T(8,128)(2,1)} %pad_maximum_fusion.3.c_ref, bf16[768,16]{1,0:T(8,128)(2,1)} %bitcast.48, bf16[2,768,3072]{2,1,0:T(8,128)(2,1)} %win_ref.7, ...), custom_call_target="tpu_custom_call" | custom-call | flops 6039797760 | bytes 11403264 | tf_op jit(solution)/shard_map/expert_rows/pallas_call | solution.py:267
  113.0 6.0 %all-to-all-start.6 = ((bf16[8,40,768]{2,1,0:T(8,128)(2,1)}), bf16[8,40,768]{2,1,0:T(8,128)(2,1)S(1)}, u32[]{:S(2)}, u32[]{:S(2)}) async-start(bf16[8,40,768]{2,1,0:T(8,128)(2,1)} %bitcast.54), calls=%async_computation.6 | async-start | bytes 983040 | tf_op jit(solution)/shard_map/all_to_all | solution.py:587
  119.0 13.4 %expert_rows.3 = (bf16[320,768]{1,0:T(8,128)(2,1)}, bf16[320,768]{1,0:T(8,128)(2,1)}, f32[16,768]{1,0:T(8,128)}) custom-call(s32[1]{0:T(128)} %bitcast.15.num_ref, bf16[320,768]{1,0:T(8,128)(2,1)} %bitcast.43, bf16[640,768]{1,0:T(8,128)(2,1)} %pad_maximum_fusion.3.c_ref, bf16[768,16]{1,0:T(8,128)(2,1)} %bitcast.49, bf16[2,768,3072]{2,1,0:T(8,128)(2,1)} %win_ref.7, ...), custom_call_target="tpu_custom_call" | custom-call | flops 6039797760 | bytes 11403264 | tf_op jit(solution)/shard_map/expert_rows/pallas_call | solution.py:267
  132.3 0.9 all-to-all-done.6
  133.2 5.1 %all-to-all-start.7 = ((bf16[8,40,768]{2,1,0:T(8,128)(2,1)}), bf16[8,40,768]{2,1,0:T(8,128)(2,1)S(1)}, u32[]{:S(2)}, u32[]{:S(2)}) async-start(bf16[8,40,768]{2,1,0:T(8,128)(2,1)} %bitcast.55), calls=%async_computation.7 | async-start | bytes 983040 | tf_op jit(solution)/shard_map/all_to_all | solution.py:587
  138.4 0.9 copy.33.target_ref.refs_3_
  139.3 12.8 %all-to-all-done.7 = bf16[8,40,768]{2,1,0:T(8,128)(2,1)S(1)} async-done(((bf16[8,40,768]{2,1,0:T(8,128)(2,1)}), bf16[8,40,768]{2,1,0:T(8,128)(2,1)S(1)}, u32[]{:S(2)}, u32[]{:S(2)}) %all-to-all-start.7) | async-done | bytes 491552 | tf_op jit(solution)/shard_map/all_to_all | solution.py:587
  152.1 0.8 copy-done.8
  152.8 7.0 %second_norm_backward.1 = (f32[512,768]{1,0:T(8,128)}, bf16[512,768]{1,0:T(8,128)(2,1)}, bf16[768,768]{1,0:T(8,128)(2,1)}, f32[1,768]{1,0:T(1,128)}) custom-call(bf16[512,768]{1,0:T(8,128)(2,1)} %refs_0_.1, f32[512,768]{1,0:T(8,128)} %get-tuple-element.43.middle_ref.refs_1_, f32[1,768]{1,0:T(1,128)} %broadcast_in_dim.30.gain_ref.refs_2_, ...), custom_call_target="tpu_custom_call" | custom-call | flops 1711276032 | bytes 8847360 | tf_op jit(solution)/shard_map/second_norm_backward/pallas_call | solution.py:386
  159.9 21.5 %attention_backward.1 = (bf16[768,768]{1,0:T(8,128)(2,1)}, bf16[768,768]{1,0:T(8,128)(2,1)}, bf16[768,768]{1,0:T(8,128)(2,1)}, f32[12,1,1024]{2,1,0:T(1,128)}, f32[512,768]{1,0:T(8,128)}, /*index=5*/f32[1,768]{1,0:T(1,128)}) custom-call(bf16[512,768]{1,0:T(8,128)(2,1)} %tok_ref.5, f32[1,768]{1,0:T(1,128)} %broadcast_in_dim.27.gain_ref, ...), custom_call_target="tpu_custom_call" | custom-call | flops 5234491392 | bytes 22806528 | tf_op jit(solution)/shard_map/attention_backward/pallas_call | solution.py:491
  181.4 3.3 pad_maximum_fusion.2
  186.0 0.7 all-gather.12.cloned.1.call-update
  186.7 3.6 all-to-all-start.3
  191.3 13.0 %all-to-all-done.3 = bf16[8,40,768]{2,1,0:T(8,128)(2,1)S(1)} async-done(((bf16[8,40,768]{2,1,0:T(8,128)(2,1)}), bf16[8,40,768]{2,1,0:T(8,128)(2,1)S(1)}, u32[]{:S(2)}, u32[]{:S(2)}) %all-to-all-start.3) | async-done | bytes 491552 | tf_op jit(solution)/shard_map/all_to_all | solution.py:587
  204.3 3.6 all-to-all-start.5
  208.0 1.0 collective-permute-start.1
  209.1 2.7 collective-permute-done.1
  211.8 2.0 collective-permute-start.2
  213.9 1.0 collective-permute-start.6
  214.9 0.6 pad_add_fusion.3.num_ref
  215.5 2.0 collective-permute-start.3
  217.6 2.3 collective-permute-done.6
  220.0 0.6 pad_add_fusion.2.num_ref
  220.6 2.9 collective-permute-start.4
  223.5 0.8 copy-done.5
  224.3 3.7 layer_output.1
  228.1 1.5 collective-permute-start.8
  229.6 0.6 slice_reduce_fusion.1
  230.2 3.1 collective-permute-done.8
  233.4 0.7 reshape_squeeze.3
  234.1 5.3 %collective-permute-done.9 = f32[17,768]{1,0:T(8,128)S(1)} collective-permute-done((f32[17,768]{1,0:T(8,128)S(1)}, f32[17,768]{1,0:T(8,128)S(1)}, u32[]{:S(2)}, u32[]{:S(2)}) %collective-permute-start.9) | collective-permute-done | bytes 52256 | tf_op jit(solution)/shard_map/ppermute | solution.py:552
  239.4 0.7 dynamic-slice_bitcast_fusion
  240.1 0.6 slice_reduce_fusion
  240.8 23.2 %all-gather.16.cloned.1.call-done = bf16[2560,768]{1,0:T(8,128)(2,1)} async-done(((bf16[640,768]{1,0:T(8,128)(2,1)}), bf16[2560,768]{1,0:T(8,128)(2,1)}) %all-gather.16.cloned.1.call-update) | async-done | bytes 3932176 | tf_op jit(solution)/shard_map/all_gather | solution.py:595
  264.0 23.9 %all-gather.14.cloned.1.call-done.x_ref = bf16[4,320,768]{2,1,0:T(8,128)(2,1)} async-done(((bf16[1,320,768]{2,1,0:T(8,128)(2,1)}), bf16[4,320,768]{2,1,0:T(8,128)(2,1)}) %all-gather.14.cloned.1.call-update) | async-done | bytes 1966096 | tf_op jit(solution)/shard_map/all_gather | solution.py:626
  287.9 13.0 %expert_weight_grads.3 = (f32[1,768,768]{2,1,0:T(8,128)}, f32[1,768,768]{2,1,0:T(8,128)}) custom-call(s32[2]{0:T(128)} %pad_add_fusion.3.num_ref, bf16[4,320,768]{2,1,0:T(8,128)(2,1)} %all-gather.14.cloned.1.call-done.x_ref, bf16[4,640,768]{2,1,0:T(8,128)(2,1)} %bitcast.37, bf16[768,16]{1,0:T(8,128)(2,1)} %bitcast.50, bf16[2,768,3072]{2,1,0:T(8,128)(2,1)} %win_ref.7, ...), custom_call_target="tpu_custom_call" | custom-call | flops 6039797760 | bytes 11010048 | tf_op jit(solution)/shard_map/expert_weight_grads/pallas_call | solution.py:325
  300.8 10.5 %all-gather.12.cloned.1.call-done.x_ref = bf16[4,320,768]{2,1,0:T(8,128)(2,1)} async-done(((bf16[1,320,768]{2,1,0:T(8,128)(2,1)}), bf16[4,320,768]{2,1,0:T(8,128)(2,1)}) %all-gather.12.cloned.1.call-update) | async-done | bytes 1966096 | tf_op jit(solution)/shard_map/all_gather | solution.py:626
  311.3 13.1 %expert_weight_grads.2 = (f32[1,768,768]{2,1,0:T(8,128)}, f32[1,768,768]{2,1,0:T(8,128)}) custom-call(s32[2]{0:T(128)} %pad_add_fusion.2.num_ref, bf16[4,320,768]{2,1,0:T(8,128)(2,1)} %all-gather.12.cloned.1.call-done.x_ref, bf16[4,640,768]{2,1,0:T(8,128)(2,1)} %bitcast.38, bf16[768,16]{1,0:T(8,128)(2,1)} %bitcast.51, bf16[2,768,3072]{2,1,0:T(8,128)(2,1)} %win_ref.7, ...), custom_call_target="tpu_custom_call" | custom-call | flops 6039797760 | bytes 11010048 | tf_op jit(solution)/shard_map/expert_weight_grads/pallas_call | solution.py:325
  324.5 7.4 %pad_maximum_fusion = (f32[2,768,768]{2,1,0:T(8,128)}, f32[2,768,768]{2,1,0:T(8,128)}) fusion(f32[1,768,768]{2,1,0:T(8,128)S(1)} %copy-done.2, f32[1,768,768]{2,1,0:T(8,128)} %get-tuple-element.68, f32[1,768,768]{2,1,0:T(8,128)S(1)} %copy-done.3, f32[1,768,768]{2,1,0:T(8,128)} %get-tuple-element.70), kind=kLoop, calls=%fused_computation | loop fusion | flops 2359296 | bytes 18874368 | tf_op jit(solution)/shard_map/concatenate | solution.py:630
  331.9 63.3 %all-reduce.4.cloned.1.call-done = (bf16[192,2304]{1,0:T(8,128)(2,1)}, bf16[192,768]{1,0:T(8,128)(2,1)}) async-done(((bf16[192,2304]{1,0:T(8,128)(2,1)}, bf16[192,768]{1,0:T(8,128)(2,1)}), (bf16[192,2304]{1,0:T(8,128)(2,1)}, bf16[192,768]{1,0:T(8,128)(2,1)})) %all-reduce.4.cloned.1.call-update) | async-done | bytes 1179664 | tf_op jit(solution)/shard_map/psum | solution.py:643
  395.2 2.4 fusion.18
  397.7 0.9 convert_element_type.19
  (99 shorter events, 3.4 us)
Async XLA Ops:
  7.2 33.3 %copy-start = (f32[32,12]{0,1:T(8,128)S(1)}, f32[32,12]{0,1:T(8,128)}, u32[]{:S(2)}) copy-start(f32[32,12]{0,1:T(8,128)} %param.26) | copy-start | bytes 4612
  7.2 3.0 copy-start.20
  7.2 3.0 copy-start.21
  7.2 40.9 %all-gather.8.cloned.1.call-start = ((), (), s32[]{:S(2)}) async-start(), calls=%async_computation.10 | async-start | bytes 4423680 | tf_op jit(solution)/shard_map/all_gather | solution.py:572
  9.4 53.3 %all-gather.10.cloned.1.call-start = ((), (), s32[]{:S(2)}) async-start(), calls=%async_computation.11 | async-start | bytes 1474560 | tf_op jit(solution)/shard_map/all_gather | solution.py:575
  10.8 12.3 %copy-start.19 = (s32[1023]{0:T(1024)S(1)}, s32[1023]{0:T(1024)}, u32[]{:S(2)}) copy-start(s32[1023]{0:T(1024)} %param.20) | copy-start | bytes 12280
  10.8 12.5 %copy-start.14 = (s32[1,512]{1,0:T(1,128)S(1)}, s32[1,512]{1,0:T(1,128)}, u32[]{:S(2)}) copy-start(s32[1,512]{1,0:T(1,128)} %param.17) | copy-start | bytes 6148
  13.6 27.7 %copy-start.17 = (f32[768]{0:T(1024)S(1)}, f32[768]{0:T(1024)}, u32[]{:S(2)}) copy-start(f32[768]{0:T(1024)} %param.21) | copy-start | bytes 9220
  13.6 28.3 %copy-start.18 = (f32[768]{0:T(1024)S(1)}, f32[768]{0:T(1024)}, u32[]{:S(2)}) copy-start(f32[768]{0:T(1024)} %param.27) | copy-start | bytes 9220
  15.8 21.0 %all-to-all-start.2 = ((bf16[8,40,768]{2,1,0:T(8,128)(2,1)}), bf16[8,40,768]{2,1,0:T(8,128)(2,1)S(1)}, u32[]{:S(2)}, u32[]{:S(2)}) async-start(bf16[8,40,768]{2,1,0:T(8,128)(2,1)} %bitcast.9), calls=%async_computation.2 | async-start | bytes 983040 | tf_op jit(solution)/shard_map/all_to_all | solution.py:587
  36.8 32.5 %all-to-all-start.1 = ((bf16[8,40,768]{2,1,0:T(8,128)(2,1)}), bf16[8,40,768]{2,1,0:T(8,128)(2,1)S(1)}, u32[]{:S(2)}, u32[]{:S(2)}) async-start(bf16[8,40,768]{2,1,0:T(8,128)(2,1)} %bitcast.7), calls=%async_computation.1 | async-start | bytes 983040 | tf_op jit(solution)/shard_map/all_to_all | solution.py:587
  67.3 25.3 %copy-start.16 = (bf16[192,16]{0,1:T(8,128)(2,1)S(1)}, bf16[192,16]{0,1:T(8,128)(2,1)}, u32[]{:S(2)}) copy-start(bf16[192,16]{0,1:T(8,128)(2,1)} %param.28) | copy-start | bytes 18436
  88.9 24.0 %all-to-all-start.4 = ((bf16[8,40,768]{2,1,0:T(8,128)(2,1)}), bf16[8,40,768]{2,1,0:T(8,128)(2,1)S(1)}, u32[]{:S(2)}, u32[]{:S(2)}) async-start(bf16[8,40,768]{2,1,0:T(8,128)(2,1)} %bitcast.16), calls=%async_computation.4 | async-start | bytes 983040 | tf_op jit(solution)/shard_map/all_to_all | solution.py:587
  112.9 6.0 %copy-start.6 = (bf16[8,40,768]{2,1,0:T(8,128)(2,1)}, bf16[8,40,768]{2,1,0:T(8,128)(2,1)S(1)}, u32[]{:S(2)}) copy-start(bf16[8,40,768]{2,1,0:T(8,128)(2,1)S(1)} %all-to-all-done.4) | copy-start | bytes 1474564
  113.0 20.3 %all-to-all-start.6 = ((bf16[8,40,768]{2,1,0:T(8,128)(2,1)}), bf16[8,40,768]{2,1,0:T(8,128)(2,1)S(1)}, u32[]{:S(2)}, u32[]{:S(2)}) async-start(bf16[8,40,768]{2,1,0:T(8,128)(2,1)} %bitcast.54), calls=%async_computation.6 | async-start | bytes 983040 | tf_op jit(solution)/shard_map/all_to_all | solution.py:587
  119.0 19.5 %copy-start.15 = (s32[512]{0:T(512)S(1)}, s32[512]{0:T(512)}, u32[]{:S(2)}) copy-start(s32[512]{0:T(512)} %fusion.10) | copy-start | bytes 6148
  133.2 18.9 %copy-start.7 = (bf16[8,40,768]{2,1,0:T(8,128)(2,1)}, bf16[8,40,768]{2,1,0:T(8,128)(2,1)S(1)}, u32[]{:S(2)}) copy-start(bf16[8,40,768]{2,1,0:T(8,128)(2,1)S(1)} %all-to-all-done.6) | copy-start | bytes 1474564
  133.2 18.9 %all-to-all-start.7 = ((bf16[8,40,768]{2,1,0:T(8,128)(2,1)}), bf16[8,40,768]{2,1,0:T(8,128)(2,1)S(1)}, u32[]{:S(2)}, u32[]{:S(2)}) async-start(bf16[8,40,768]{2,1,0:T(8,128)(2,1)} %bitcast.55), calls=%async_computation.7 | async-start | bytes 983040 | tf_op jit(solution)/shard_map/all_to_all | solution.py:587
  138.4 102.4 %reduce-scatter.5.cloned.1.call-start = ((), (), s32[]{:S(2)}) async-start(), calls=%async_computation.13 | async-start | bytes 1474560 | tf_op jit(solution)/shard_map/reduce_scatter | solution.py:642
  152.1 0.8 copy-start.8
  159.9 80.8 %reduce-scatter.3.cloned.1.call-start = ((), (), s32[]{:S(2)}) async-start(), calls=%async_computation.12 | async-start | bytes 4423680 | tf_op jit(solution)/shard_map/reduce_scatter | solution.py:642
  184.8 5.9 %copy-start.22 = (f32[12,1,1024]{2,1,0:T(1,128)S(1)}, f32[12,1,1024]{2,1,0:T(1,128)}, u32[]{:S(2)}) copy-start(f32[12,1,1024]{2,1,0:T(1,128)} %get-tuple-element.60) | copy-start | bytes 147460
  184.8 6.3 %copy-start.12 = (f32[1,768]{1,0:T(1,128)S(1)}, f32[1,768]{1,0:T(1,128)}, u32[]{:S(2)}) copy-start(f32[1,768]{1,0:T(1,128)} %get-tuple-element.59) | copy-start | bytes 9220
  184.8 6.4 %copy-start.10 = (f32[16,768]{1,0:T(8,128)S(1)}, f32[16,768]{1,0:T(8,128)}, u32[]{:S(2)}) copy-start(f32[16,768]{1,0:T(8,128)} %get-tuple-element.65) | copy-start | bytes 147460
  184.8 6.4 %copy-start.11 = (f32[16,768]{1,0:T(8,128)S(1)}, f32[16,768]{1,0:T(8,128)}, u32[]{:S(2)}) copy-start(f32[16,768]{1,0:T(8,128)} %get-tuple-element.66) | copy-start | bytes 147460
  184.8 24.2 %copy-start.13 = (f32[1,768]{1,0:T(1,128)S(1)}, f32[1,768]{1,0:T(1,128)}, u32[]{:S(2)}) copy-start(f32[1,768]{1,0:T(1,128)} %get-tuple-element.67) | copy-start | bytes 9220
  184.8 79.2 %all-gather.16.cloned.1.call-start = ((), (), s32[]{:S(2)}) async-start(), calls=%async_computation.16 | async-start | bytes 4915200 | tf_op jit(solution)/shard_map/all_gather | solution.py:595
  185.4 102.5 %all-gather.14.cloned.1.call-start = ((), (), s32[]{:S(2)}) async-start(), calls=%async_computation.15 | async-start | bytes 2457600 | tf_op jit(solution)/shard_map/all_gather | solution.py:626
  186.0 125.3 %all-gather.12.cloned.1.call-start = ((), (), s32[]{:S(2)}) async-start(), calls=%async_computation.14 | async-start | bytes 2457600 | tf_op jit(solution)/shard_map/all_gather | solution.py:626
  186.7 17.6 %all-to-all-start.3 = ((bf16[8,40,768]{2,1,0:T(8,128)(2,1)}), bf16[8,40,768]{2,1,0:T(8,128)(2,1)S(1)}, u32[]{:S(2)}, u32[]{:S(2)}) async-start(bf16[8,40,768]{2,1,0:T(8,128)(2,1)} %bitcast.13), calls=%async_computation.3 | async-start | bytes 983040 | tf_op jit(solution)/shard_map/all_to_all | solution.py:587
  191.1 16.9 %collective-permute-start = (f32[2,768]{1,0:T(2,128)S(1)}, f32[2,768]{1,0:T(2,128)S(1)}, u32[]{:S(2)}, u32[]{:S(2)}) collective-permute-start(f32[2,768]{1,0:T(2,128)S(1)} %fusion.6), channel_id=1, source_target_pairs={{0,8},{8,0},{16,24},{24,16},{1,9},{9,1},{17,25},{25,17},{2,10},{10... | collective-permute-start | bytes 18440 | tf_op jit(solution)/shard_map/ppermute | solution.py:552
  204.3 19.2 %copy-start.4 = (bf16[8,40,768]{2,1,0:T(8,128)(2,1)}, bf16[8,40,768]{2,1,0:T(8,128)(2,1)S(1)}, u32[]{:S(2)}) copy-start(bf16[8,40,768]{2,1,0:T(8,128)(2,1)S(1)} %all-to-all-done.3) | copy-start | bytes 1474564
  204.3 19.2 %all-to-all-start.5 = ((bf16[8,40,768]{2,1,0:T(8,128)(2,1)}), bf16[8,40,768]{2,1,0:T(8,128)(2,1)S(1)}, u32[]{:S(2)}, u32[]{:S(2)}) async-start(bf16[8,40,768]{2,1,0:T(8,128)(2,1)} %bitcast.18), calls=%async_computation.5 | async-start | bytes 983040 | tf_op jit(solution)/shard_map/all_to_all | solution.py:587
  207.9 187.3 %all-reduce.4.cloned.1.call-start = ((), (), s32[]{:S(2)}) async-start(), calls=%async_computation.17 | async-start | bytes 2359296 | tf_op jit(solution)/shard_map/psum | solution.py:643
  208.0 3.8 collective-permute-start.1
  209.0 4.9 %collective-permute-start.5 = (f32[17,768]{1,0:T(8,128)S(1)}, f32[17,768]{1,0:T(8,128)S(1)}, u32[]{:S(2)}, u32[]{:S(2)}) collective-permute-start(f32[17,768]{1,0:T(8,128)S(1)} %pad_maximum_fusion.5), channel_id=1, source_target_pairs={{0,8},{8,0},{16,24},{24,16},{1,9},{9,1},{17,25},{25,17},{2,10},{10... | collective-permute-start | bytes 156680 | tf_op jit(solution)/shard_map/ppermute | solution.py:552
  211.8 3.7 collective-permute-start.2
  213.9 6.0 %collective-permute-start.6 = (f32[17,768]{1,0:T(8,128)S(1)}, f32[17,768]{1,0:T(8,128)S(1)}, u32[]{:S(2)}, u32[]{:S(2)}) collective-permute-start(f32[17,768]{1,0:T(8,128)S(1)} %fusion.14), channel_id=1, source_target_pairs={{0,16},{8,24},{16,0},{24,8},{1,17},{9,25},{17,1},{25,9},{2,18},{10... | collective-permute-start | bytes 156680 | tf_op jit(solution)/shard_map/ppermute | solution.py:552
  215.5 5.1 %collective-permute-start.3 = (f32[2,768]{1,0:T(2,128)S(1)}, f32[2,768]{1,0:T(2,128)S(1)}, u32[]{:S(2)}, u32[]{:S(2)}) collective-permute-start(f32[2,768]{1,0:T(2,128)S(1)} %add.69), channel_id=1, source_target_pairs={{0,2},{1,3},{2,0},{3,1},{4,6},{5,7},{6,4},{7,5},{8,10},{9,11},{10,... | collective-permute-start | bytes 18440 | tf_op jit(solution)/shard_map/ppermute | solution.py:552
  219.9 8.2 %collective-permute-start.7 = (f32[17,768]{1,0:T(8,128)S(1)}, f32[17,768]{1,0:T(8,128)S(1)}, u32[]{:S(2)}, u32[]{:S(2)}) collective-permute-start(f32[17,768]{1,0:T(8,128)S(1)} %add.74), channel_id=1, source_target_pairs={{0,1},{1,0},{2,3},{3,2},{4,5},{5,4},{6,7},{7,6},{8,9},{9,8},{10,11... | collective-permute-start | bytes 156680 | tf_op jit(solution)/shard_map/ppermute | solution.py:552
  220.6 7.4 %collective-permute-start.4 = (f32[2,768]{1,0:T(2,128)S(1)}, f32[2,768]{1,0:T(2,128)S(1)}, u32[]{:S(2)}, u32[]{:S(2)}) collective-permute-start(f32[2,768]{1,0:T(2,128)S(1)} %add.70), channel_id=1, source_target_pairs={{0,4},{1,5},{2,6},{3,7},{4,0},{5,1},{6,2},{7,3},{8,12},{9,13},{10,... | collective-permute-start | bytes 18440 | tf_op jit(solution)/shard_map/ppermute | solution.py:552
  223.5 0.8 copy-start.5
  228.1 5.2 %collective-permute-start.8 = (f32[17,768]{1,0:T(8,128)S(1)}, f32[17,768]{1,0:T(8,128)S(1)}, u32[]{:S(2)}, u32[]{:S(2)}) collective-permute-start(f32[17,768]{1,0:T(8,128)S(1)} %add.75), channel_id=1, source_target_pairs={{0,2},{1,3},{2,0},{3,1},{4,6},{5,7},{6,4},{7,5},{8,10},{9,11},{10,... | collective-permute-start | bytes 156680 | tf_op jit(solution)/shard_map/ppermute | solution.py:552
  233.3 6.1 %collective-permute-start.9 = (f32[17,768]{1,0:T(8,128)S(1)}, f32[17,768]{1,0:T(8,128)S(1)}, u32[]{:S(2)}, u32[]{:S(2)}) collective-permute-start(f32[17,768]{1,0:T(8,128)S(1)} %add.76), channel_id=1, source_target_pairs={{0,4},{1,5},{2,6},{3,7},{4,0},{5,1},{6,2},{7,3},{8,12},{9,13},{10,... | collective-permute-start | bytes 156680 | tf_op jit(solution)/shard_map/ppermute | solution.py:552
  300.8 23.6 %copy-start.2 = (f32[1,768,768]{2,1,0:T(8,128)S(1)}, f32[1,768,768]{2,1,0:T(8,128)}, u32[]{:S(2)}) copy-start(f32[1,768,768]{2,1,0:T(8,128)} %get-tuple-element.69) | copy-start | bytes 7077892
  311.3 13.2 %copy-start.3 = (f32[1,768,768]{2,1,0:T(8,128)S(1)}, f32[1,768,768]{2,1,0:T(8,128)}, u32[]{:S(2)}) copy-start(f32[1,768,768]{2,1,0:T(8,128)} %get-tuple-element.71) | copy-start | bytes 7077892
  324.5 74.0 %copy-start.1 = (f32[32,12]{0,1:T(8,128)S(1)}, f32[32,12]{0,1:T(8,128)}, u32[]{:S(2)}) copy-start(f32[32,12]{0,1:T(8,128)} %param.26) | copy-start | bytes 4612
  395.2 2.4 copy-start.9
Sparse Core Ops, SparseCore 0:
  10.2 33.4 all-gather.7
  45.2 17.4 all-gather.9
  160.0 24.1 reduce-scatter.4
  187.4 42.1 reduce-scatter.2
  231.0 32.9 all-gather.15
  266.0 21.8 all-gather.13
  289.4 21.8 all-gather.11
  314.9 80.3 all-reduce.3
